TPU v7x, 512 devices: a whole 4x4x16 slice. The times are simulated.
512 devices in a mesh: tile: 128 (over x, y_lo, z), kern: 4 (over y_hi, core).
Axes of the slice: x: 4, y: 4 (y_hi: 2, y_lo: 2; y = y_hi * 2 + y_lo), z: 16, core: 2. Of those that a mesh axis runs over, the one named last changes fastest.
Arguments:
- mask_logit: float32 [16384, 256], P('tile'), may hold values from -6 to 6
- target: int32 [16384, 256], P('tile'), may hold values 0 or 1
- kern_real: float32 [12, 65, 65], P('kern'), may hold values from -0.09375 to 0.09375
- kern_imag: float32 [12, 65, 65], P('kern'), may hold values from -0.09375 to 0.09375
- kern_weight: float32 [12], P('kern'), may hold values from 0.07 to 0.14
Outputs:
- logit_grad: float32 [16384, 256], P('tile', 'kern')
All inputs are finite; a program needn't handle non-finite values. No bound on the sum of `target` on one device may be relied on, other than what follows from the above.
Results may differ from a plain program's by a relative error of at most 0.00021.
Values sent between devices are 32-bit elements; how exact they have to be, the bound alone decides.
A program may use at most 64 MiB of HBM per device.

v0:
```python
import functools
import math

import jax
import jax.numpy as jnp
import ml_dtypes
import numpy as np
from jax import lax
from jax.experimental import pallas as pl
from jax.experimental.pallas import tpu as pltpu
from jax.sharding import PartitionSpec as P

F32 = jnp.float32
BF16 = jnp.bfloat16
MESH = pl.DeviceIdType.MESH

BAND = 128
COLS = 256
TAPS = 65
RADIUS = 32
OWN = 3
BOTH = 2 * OWN
NX = 224
FX = NX // 2
NY = 256
FIELD = 160
FROWS = 192


def pair(table):
    high = table.astype(ml_dtypes.bfloat16)
    low = (table - high.astype(np.float64)).astype(ml_dtypes.bfloat16)
    return np.stack([high, low])


def tables():
    theta = 2.0 * np.pi * (np.arange(FX) + 0.5) / NX

    def wave(offsets):
        angle = theta[:, None] * offsets[None, :]
        return np.concatenate([np.cos(angle), -np.sin(angle)], 0)

    scale = 2.0 / (NX * NY)
    into, back_in, out, last, pick = [], [], [], [], []
    for half in range(2):
        local = np.arange(COLS) - 64 * half
        full = wave(local) * ((local >= 0) & (local < 192))[None, :]
        into.append(pair(full))
        part = full[:, 96 * half : 96 * half + FIELD]
        back_in.append(pair(part))
        out.append(pair(scale * part.T))
        for core in range(2):
            cols = np.concatenate([64 * (2 * half + c) + np.arange(64) for c in (core, 1 - core)])
            last.append(pair(2.0 * scale * full[:, cols].T))
        pick.append((np.arange(COLS)[None, :] == np.arange(FIELD)[:, None] + 96 * half))
    taps = wave(np.arange(64) - RADIUS)
    zero = np.zeros_like(taps)
    taps = np.concatenate([np.concatenate([taps, zero], 1), np.concatenate([zero, taps], 1)], 0)
    edge = np.broadcast_to(wave(np.array([RADIUS])), (NX, 128))
    rows = []
    for odd in range(2):
        angle = 2.0 * np.pi * np.arange(128)[:, None] * (2 * np.arange(128) + odd)[None, :] / NY
        c, s = np.cos(angle), np.sin(angle)
        rows.append(pair(np.concatenate([np.concatenate([c, -s], 1), np.concatenate([s, c], 1)], 0)))
    return dict(
        rows=np.stack(rows),
        into=np.stack(into),
        taps=pair(taps),
        edge=edge.astype(np.float32),
        out=np.stack(out),
        back_in=np.stack(back_in),
        last=np.stack(last),
        pick=np.stack(pick).astype(ml_dtypes.bfloat16),
    )


NAMES = ("taps", "edge", "rows", "into", "out", "pick", "back_in", "last")


def split(value):
    high = value.astype(BF16)
    return high, (value - high.astype(F32)).astype(BF16)


def dot(left, right):
    return jnp.dot(left, right, preferred_element_type=F32)


def dot_t(left, right):
    return lax.dot_general(left, right, (((1,), (1,)), ((), ())), preferred_element_type=F32)


def right_mul(value, table, mul):
    high, low = split(value)
    count = value.shape[0]
    both = mul(jnp.concatenate([high, low], 0), table[0])
    return both[:count] + both[count:] + mul(high, table[1])


def left_mul(table, value, mul):
    high, low = split(value)
    return mul(table[0], high) + mul(table[1], high) + mul(table[0], low)


def kernel(
    logit, target, kern_real, kern_imag, weight, taps_h, edge_h, rows_h, into_h, out_h, pick_h, back_h, last_h,
    result,
    ext, goal, kr, ki, w, taps_c, edge_c, rows_c, into_c, out_c, pick_c, back_c, last_c,
    packed, spec, fields, part, part_in, grad, grad_in,
    local_sem, send_sem, recv_sem,
):
    tile, kern = lax.axis_index("tile"), lax.axis_index("kern")
    tiles = lax.axis_size("tile")
    half, core = kern // 2, lax.rem(kern, 2)
    before = {"tile": lax.rem(tile + tiles - 1, tiles)}
    after = {"tile": lax.rem(tile + 1, tiles)}
    mate = {"kern": 2 * half + (1 - core)}
    across = {"kern": 2 * (1 - half) + core}

    barrier = pltpu.get_barrier_semaphore()
    for device in (before, after, across, mate):
        pl.semaphore_signal(barrier, inc=1, device_id=device, device_id_type=MESH)

    pairs = (
        (kern_real, kr),
        (kern_imag, ki),
        (weight, w),
        (taps_h, taps_c),
        (edge_h, edge_c),
        (rows_h, rows_c),
        (logit, ext.at[pl.ds(64, BAND)]),
        (into_h.at[half], into_c),
        (out_h.at[half], out_c),
        (target, goal.at[pl.ds(RADIUS, BAND)]),
        (pick_h.at[half], pick_c),
        (back_h.at[half], back_c),
        (last_h.at[kern], last_c),
    )
    loads = [pltpu.make_async_copy(src, dst, local_sem.at[i]) for i, (src, dst) in enumerate(pairs)]
    for load in loads:
        load.start()

    def send(index, src, dst, device):
        copy = pltpu.make_async_remote_copy(
            src_ref=src, dst_ref=dst, send_sem=send_sem.at[index], recv_sem=recv_sem.at[index],
            device_id=device, device_id_type=MESH,
        )
        copy.start()
        return copy

    for load in loads[:3]:
        load.wait()
    eye = lax.broadcasted_iota(jnp.int32, (TAPS, 128), 0) == lax.broadcasted_iota(jnp.int32, (TAPS, 128), 1)
    ends = []
    for k in range(OWN):
        factor = jnp.sqrt(jnp.full((TAPS, TAPS), w[k], F32))
        real, imag = kr[k] * factor, ki[k] * factor
        packed[k, 0:72, :] = jnp.zeros((72, 128), F32)
        packed[k, 0:TAPS, :] = jnp.concatenate([real[:, 0:64], imag[:, 0:64]], axis=1)
        for grid in (real, imag):
            column = jnp.broadcast_to(grid[:, 64:65], (TAPS, 128))
            ends.append(jnp.sum(jnp.where(eye, column, 0.0), axis=0, keepdims=True))
    row_id = lax.broadcasted_iota(jnp.int32, (8, 128), 0)
    end_rows = jnp.zeros((8, 128), F32)
    for i, end in enumerate(ends):
        end_rows = jnp.where(row_id == i, jnp.broadcast_to(end, (8, 128)), end_rows)
    packed[OWN, 0:72, :] = jnp.zeros((72, 128), F32)
    packed[OWN, 0:8, :] = end_rows

    pl.semaphore_wait(barrier, 4)
    sends = [
        send(0, packed.at[pl.ds(0, OWN + 1)], packed.at[pl.ds(OWN + 1, OWN + 1)], across),
        send(1, logit.at[pl.ds(64, 64)], ext.at[pl.ds(0, 64)], after),
        send(2, logit.at[pl.ds(0, 64)], ext.at[pl.ds(192, 64)], before),
        send(3, target.at[pl.ds(96, RADIUS)], goal.at[pl.ds(0, RADIUS)], after),
        send(4, target.at[pl.ds(0, RADIUS)], goal.at[pl.ds(160, RADIUS)], before),
    ]

    def butterfly(value):
        real0, real1 = value[:FX, :128], value[:FX, 128:]
        imag0, imag1 = value[FX:, :128], value[FX:, 128:]
        even = jnp.concatenate([real0 + real1, imag0 + imag1], 1)
        odd = jnp.concatenate([real0 - real1, imag0 - imag1], 1)
        return even, odd

    def spectrum(group):
        base = group * (OWN + 1)
        ends = packed[base + OWN, 0:8, :]
        edge = edge_c[...]
        for k in range(OWN):
            taps = jnp.concatenate([packed[base + k], jnp.zeros((56, 128), F32)], 0)
            half_way = left_mul((taps_c[0], taps_c[1]), taps, dot_t)
            stacked = []
            for part_id in range(2):
                row = ends[2 * k + part_id : 2 * k + part_id + 1, :]
                own = half_way[NX * part_id : NX * (part_id + 1)] + edge * row
                stacked.append(jnp.concatenate([own[:FX], own[FX:]], 1))
            value = jnp.concatenate(stacked, 0)
            for odd in range(2):
                spec[group * OWN + k, :, 256 * odd : 256 * odd + 256] = right_mul(
                    value, (rows_c[odd, 0], rows_c[odd, 1]), dot
                )

    for load in loads[3:6]:
        load.wait()
    spectrum(0)

    for load in loads[6:9]:
        load.wait()
    sends[1].wait()
    sends[2].wait()
    row = lax.broadcasted_iota(jnp.int32, (NY, COLS), 0) - 64 + tile * BAND
    mask = jnp.where((row >= 0) & (row < tiles * BAND), jax.nn.sigmoid(3.0 * ext[...]), 0.0)
    even, odd = butterfly(left_mul((into_c[0], into_c[1]), mask, dot_t))
    mask_spec = (
        right_mul(even, (rows_c[0, 0], rows_c[0, 1]), dot),
        right_mul(odd, (rows_c[1, 0], rows_c[1, 1]), dot),
    )

    def forward(k):
        ends = []
        for odd in range(2):
            mr, mi = mask_spec[odd][:, :128], mask_spec[odd][:, 128:]
            rows = []
            for c in range(2):
                sr = spec[k, FX * c : FX * (c + 1), 256 * odd : 256 * odd + 128]
                si = spec[k, FX * c : FX * (c + 1), 256 * odd + 128 : 256 * odd + 256]
                rows.append(jnp.concatenate([sr * mr + si * mi, sr * mi - si * mr], 1))
            ends.append(right_mul(jnp.concatenate(rows, 0), (rows_c[odd, 0], rows_c[odd, 1]), dot_t))
        plus, minus = ends[0] + ends[1], ends[0] - ends[1]
        total = None
        for c in range(2):
            rows = slice(FX * c, FX * (c + 1))
            wave = jnp.concatenate(
                [
                    jnp.concatenate([plus[rows, :128], minus[rows, :128]], 1),
                    jnp.concatenate([plus[rows, 128:], minus[rows, 128:]], 1),
                ],
                0,
            )
            field = left_mul((out_c[0], out_c[1]), wave, dot)
            fields[2 * k + c] = field
            total = field * field if total is None else total + field * field
        return total

    inten = None
    for k in range(BOTH):
        if k == OWN:
            sends[0].wait()
            spectrum(1)
        own = forward(k)
        inten = own if inten is None else inten + own
    part[...] = inten
    swap = send(5, part, part_in, mate)

    sends[3].wait()
    sends[4].wait()
    for load in loads[9:]:
        load.wait()
    goal_t = dot_t(pick_c[...], goal[...].astype(F32).astype(BF16))

    swap.wait()
    printed = jax.nn.sigmoid(6.0 * (part[...] + part_in[...] - 1.0))
    goal_t = jnp.concatenate([goal_t, jnp.zeros((FIELD, NY - FROWS), F32)], 1)
    slope = 12.0 * (printed - goal_t) * printed * (1.0 - printed)
    lane = lax.broadcasted_iota(jnp.int32, (FIELD, NY), 1)
    place = lane - RADIUS + tile * BAND
    slope = jnp.where((lane < FROWS) & (place >= 0) & (place < tiles * BAND), slope, 0.0)

    acc = [None, None]
    for k in range(BOTH):
        evens, odds = [], []
        for c in range(2):
            source = slope * fields[2 * k + c]
            even, odd = butterfly(left_mul((back_c[0], back_c[1]), source, dot))
            evens.append(even)
            odds.append(odd)
        for odd, values in enumerate((evens, odds)):
            wave = right_mul(jnp.concatenate(values, 0), (rows_c[odd, 0], rows_c[odd, 1]), dot)
            for c in range(2):
                rows = slice(FX * c, FX * (c + 1))
                sr = spec[k, FX * c : FX * (c + 1), 256 * odd : 256 * odd + 128]
                si = spec[k, FX * c : FX * (c + 1), 256 * odd + 128 : 256 * odd + 256]
                gr, gi = wave[rows, :128], wave[rows, 128:]
                real, imag = sr * gr - si * gi, sr * gi + si * gr
                if acc[odd] is None:
                    acc[odd] = (real, imag)
                else:
                    acc[odd] = (acc[odd][0] + real, acc[odd][1] + imag)

    sign = 1.0 - 2.0 * lax.rem(lax.broadcasted_iota(jnp.int32, (FX, 128), 1), 2).astype(F32)
    even = jnp.concatenate([acc[0][0] * sign, acc[0][1] * sign], 1)
    odd = jnp.concatenate([-acc[1][1] * sign, acc[1][0] * sign], 1)
    back = right_mul(even, (rows_c[0, 0], rows_c[0, 1]), dot_t) + right_mul(odd, (rows_c[1, 0], rows_c[1, 1]), dot_t)
    back = jnp.concatenate([back[:, :128], back[:, 128:]], 0)
    grad[...] = left_mul((last_c[0], last_c[1]), back, dot)
    swap_2 = send(6, grad.at[pl.ds(64, 64)], grad_in, mate)

    own = jax.nn.sigmoid(3.0 * ext[64 : 64 + BAND, :])
    own = jnp.where(half == 0, own[:, :128], own[:, 128:])
    own = jnp.where(core == 0, own[:, :64], own[:, 64:])
    factor = 3.0 * own * (1.0 - own)
    swap_2.wait()
    total = grad[0:64, :] + grad_in[...]
    result[...] = jnp.transpose(total) * factor


def body(consts, mask_logit, target, kern_real, kern_imag, kern_weight):
    any_spec = pl.BlockSpec(memory_space=pl.ANY)
    vm = pltpu.VMEM
    scratch = [
        vm((NY, COLS), F32),
        vm((FROWS, COLS), jnp.int32),
        vm((OWN, TAPS, TAPS), F32),
        vm((OWN, TAPS, TAPS), F32),
        pltpu.SMEM((OWN,), F32),
        vm((2, 2 * NX, 128), BF16),
        vm((NX, 128), F32),
        vm((2, 2, 256, 256), BF16),
        vm((2, NX, COLS), BF16),
        vm((2, FIELD, NX), BF16),
        vm((FIELD, COLS), BF16),
        vm((2, NX, FIELD), BF16),
        vm((2, 128, NX), BF16),
        vm((2 * (OWN + 1), 72, 128), F32),
        vm((BOTH, 2 * FX, 512), F32),
        vm((2 * BOTH, FIELD, NY), F32),
        vm((FIELD, NY), F32),
        vm((FIELD, NY), F32),
        vm((128, BAND), F32),
        vm((64, BAND), F32),
        pltpu.SemaphoreType.DMA((13,)),
        pltpu.SemaphoreType.DMA((7,)),
        pltpu.SemaphoreType.DMA((7,)),
    ]
    return pl.pallas_call(
        kernel,
        out_shape=jax.ShapeDtypeStruct((BAND, 64), F32),
        in_specs=[any_spec] * (5 + len(NAMES)),
        out_specs=pl.BlockSpec(memory_space=pltpu.VMEM),
        scratch_shapes=scratch,
        compiler_params=pltpu.CompilerParams(
            collective_id=0, has_side_effects=True, vmem_limit_bytes=48 * 2**20
        ),
    )(mask_logit, target, kern_real, kern_imag, kern_weight, *consts)


def solution(mesh):
    made = tables()
    consts = [made[name] for name in NAMES]
    in_specs = (
        P("tile", None),
        P("tile", None),
        P("kern", None, None),
        P("kern", None, None),
        P("kern"),
    )
    mapped = jax.shard_map(
        lambda *args: body([jnp.asarray(c) for c in consts], *args),
        mesh=mesh, in_specs=in_specs, out_specs=P("tile", "kern"), check_vma=False,
    )
    return mapped
```

profile of v0, /device:TPU:1, one launch (start us, length us, event | category | flops | bytes accessed | tf_op | source)
XLA Modules:
  0.0 44.3 jit_solution(296774319407546352)
XLA Ops:
  0.0 0.0 copy-start
  0.0 1.0 %copy-done = bf16[4,2,128,224]{3,2,1,0:T(8,128)(2,1)S(1)} copy-done((bf16[4,2,128,224]{3,2,1,0:T(8,128)(2,1)S(1)}, bf16[4,2,128,224]{3,2,1,0:T(8,128)(2,1)}, u32[]{:S(2)}) %copy-start) | copy-done | bytes 458776
  1.0 0.0 copy-start.1
  1.0 1.0 %copy-done.1 = bf16[2,2,256,256]{3,2,1,0:T(8,128)(2,1)S(1)} copy-done((bf16[2,2,256,256]{3,2,1,0:T(8,128)(2,1)S(1)}, bf16[2,2,256,256]{3,2,1,0:T(8,128)(2,1)}, u32[]{:S(2)}) %copy-start.1) | copy-done | bytes 524312
  2.1 0.0 copy-start.2
  2.1 1.0 %copy-done.2 = bf16[2,2,224,160]{3,2,1,0:T(8,128)(2,1)S(1)} copy-done((bf16[2,2,224,160]{3,2,1,0:T(8,128)(2,1)S(1)}, bf16[2,2,224,160]{3,2,1,0:T(8,128)(2,1)}, u32[]{:S(2)}) %copy-start.2) | copy-done | bytes 286744
  3.1 0.0 copy-start.3
  3.1 1.0 %copy-done.3 = bf16[2,2,224,256]{3,2,1,0:T(8,128)(2,1)S(1)} copy-done((bf16[2,2,224,256]{3,2,1,0:T(8,128)(2,1)S(1)}, bf16[2,2,224,256]{3,2,1,0:T(8,128)(2,1)}, u32[]{:S(2)}) %copy-start.3) | copy-done | bytes 458776
  4.1 0.0 copy-start.4
  4.1 1.0 %copy-done.4 = bf16[2,2,160,224]{3,2,1,0:T(8,128)(2,1)S(1)} copy-done((bf16[2,2,160,224]{3,2,1,0:T(8,128)(2,1)S(1)}, bf16[2,2,160,224]{3,2,1,0:T(8,128)(2,1)}, u32[]{:S(2)}) %copy-start.4) | copy-done | bytes 286744
  5.1 0.0 copy-start.5
  5.1 0.9 %copy-done.5 = bf16[2,448,128]{2,1,0:T(8,128)(2,1)S(1)} copy-done((bf16[2,448,128]{2,1,0:T(8,128)(2,1)S(1)}, bf16[2,448,128]{2,1,0:T(8,128)(2,1)}, u32[]{:S(2)}) %copy-start.5) | copy-done | bytes 229400
  6.0 0.0 copy-start.6
  6.0 0.9 %copy-done.6 = bf16[2,160,256]{2,1,0:T(8,128)(2,1)S(1)} copy-done((bf16[2,160,256]{2,1,0:T(8,128)(2,1)S(1)}, bf16[2,160,256]{2,1,0:T(8,128)(2,1)}, u32[]{:S(2)}) %copy-start.6) | copy-done | bytes 163864
  7.0 0.0 copy-start.7
  7.0 0.9 %copy-done.7 = f32[128,256]{1,0:T(8,128)S(1)} copy-done((f32[128,256]{1,0:T(8,128)S(1)}, f32[128,256]{1,0:T(8,128)}, u32[]{:S(2)}) %copy-start.7) | copy-done | bytes 131096
  7.9 0.0 copy-start.8
  7.9 0.9 %copy-done.8 = s32[128,256]{1,0:T(8,128)S(1)} copy-done((s32[128,256]{1,0:T(8,128)S(1)}, s32[128,256]{1,0:T(8,128)}, u32[]{:S(2)}) %copy-start.8) | copy-done | bytes 131096
  8.8 0.0 copy-start.9
  8.8 0.9 %copy-done.9 = f32[224,128]{1,0:T(8,128)S(1)} copy-done((f32[224,128]{1,0:T(8,128)S(1)}, f32[224,128]{1,0:T(8,128)}, u32[]{:S(2)}) %copy-start.9) | copy-done | bytes 114712
  9.7 0.0 copy-start.10
  9.7 0.9 %copy-done.10 = f32[3,65,65]{2,1,0:T(8,128)S(1)} copy-done((f32[3,65,65]{2,1,0:T(8,128)S(1)}, f32[3,65,65]{2,1,0:T(8,128)}, u32[]{:S(2)}) %copy-start.10) | copy-done | bytes 50724
  10.6 0.0 copy-start.11
  10.6 0.9 %copy-done.11 = f32[3,65,65]{2,1,0:T(8,128)S(1)} copy-done((f32[3,65,65]{2,1,0:T(8,128)S(1)}, f32[3,65,65]{2,1,0:T(8,128)}, u32[]{:S(2)}) %copy-start.11) | copy-done | bytes 50724
  11.5 0.0 copy-start.12
  11.5 0.7 %copy-done.12 = f32[3]{0:T(128)S(1)} copy-done((f32[3]{0:T(128)S(1)}, f32[3]{0:T(128)}, u32[]{:S(2)}) %copy-start.12) | copy-done | bytes 36
  12.1 31.5 %shard_map.127 = f32[128,64]{1,0:T(8,128)S(1)} custom-call(f32[128,256]{1,0:T(8,128)S(1)} %copy-done.7, s32[128,256]{1,0:T(8,128)S(1)} %copy-done.8, f32[3,65,65]{2,1,0:T(8,128)S(1)} %copy-done.10, f32[3,65,65]{2,1,0:T(8,128)S(1)} %copy-done.11, f32[3]{0:T(128)S(1)} %copy-done.12, bf16[2,448,128]{2,1,0:T(8,128)(2,1)S(1)} %copy-done.5, ...), custom_call_target="tpu_custom_call" | custom-call | tf_op jit(solution)/shard_map/pallas_call | solution.py:336
  43.6 0.7 %copy.14 = f32[128,64]{0,1:T(8,128)} copy(f32[128,64]{1,0:T(8,128)S(1)} %shard_map.127) | data formatting | bytes 65536 | tf_op jit(solution)/shard_map/pallas_call | solution.py:336
Async XLA Ops:
  0.0 1.0 %copy-start = (bf16[4,2,128,224]{3,2,1,0:T(8,128)(2,1)S(1)}, bf16[4,2,128,224]{3,2,1,0:T(8,128)(2,1)}, u32[]{:S(2)}) copy-start(bf16[4,2,128,224]{3,2,1,0:T(8,128)(2,1)} %constant.23.clone.last_h) | copy-start | bytes 1376260
  1.0 1.0 %copy-start.1 = (bf16[2,2,256,256]{3,2,1,0:T(8,128)(2,1)S(1)}, bf16[2,2,256,256]{3,2,1,0:T(8,128)(2,1)}, u32[]{:S(2)}) copy-start(bf16[2,2,256,256]{3,2,1,0:T(8,128)(2,1)} %constant.18.clone.rows_h) | copy-start | bytes 1572868
  2.1 1.0 %copy-start.2 = (bf16[2,2,224,160]{3,2,1,0:T(8,128)(2,1)S(1)}, bf16[2,2,224,160]{3,2,1,0:T(8,128)(2,1)}, u32[]{:S(2)}) copy-start(bf16[2,2,224,160]{3,2,1,0:T(8,128)(2,1)} %constant.22.clone.back_h) | copy-start | bytes 860164
  3.1 1.0 %copy-start.3 = (bf16[2,2,224,256]{3,2,1,0:T(8,128)(2,1)S(1)}, bf16[2,2,224,256]{3,2,1,0:T(8,128)(2,1)}, u32[]{:S(2)}) copy-start(bf16[2,2,224,256]{3,2,1,0:T(8,128)(2,1)} %constant.19.clone.into_h) | copy-start | bytes 1376260
  4.1 1.0 %copy-start.4 = (bf16[2,2,160,224]{3,2,1,0:T(8,128)(2,1)S(1)}, bf16[2,2,160,224]{3,2,1,0:T(8,128)(2,1)}, u32[]{:S(2)}) copy-start(bf16[2,2,160,224]{3,2,1,0:T(8,128)(2,1)} %constant.20.clone.out_h) | copy-start | bytes 860164
  5.1 0.9 %copy-start.5 = (bf16[2,448,128]{2,1,0:T(8,128)(2,1)S(1)}, bf16[2,448,128]{2,1,0:T(8,128)(2,1)}, u32[]{:S(2)}) copy-start(bf16[2,448,128]{2,1,0:T(8,128)(2,1)} %constant.16.clone.taps_h) | copy-start | bytes 688132
  6.0 0.9 %copy-start.6 = (bf16[2,160,256]{2,1,0:T(8,128)(2,1)S(1)}, bf16[2,160,256]{2,1,0:T(8,128)(2,1)}, u32[]{:S(2)}) copy-start(bf16[2,160,256]{2,1,0:T(8,128)(2,1)} %constant.21.clone.pick_h) | copy-start | bytes 491524
  7.0 0.9 %copy-start.7 = (f32[128,256]{1,0:T(8,128)S(1)}, f32[128,256]{1,0:T(8,128)}, u32[]{:S(2)}) copy-start(f32[128,256]{1,0:T(8,128)} %logit.1) | copy-start | bytes 393220
  7.9 0.9 %copy-start.8 = (s32[128,256]{1,0:T(8,128)S(1)}, s32[128,256]{1,0:T(8,128)}, u32[]{:S(2)}) copy-start(s32[128,256]{1,0:T(8,128)} %target.1) | copy-start | bytes 393220
  8.8 0.9 %copy-start.9 = (f32[224,128]{1,0:T(8,128)S(1)}, f32[224,128]{1,0:T(8,128)}, u32[]{:S(2)}) copy-start(f32[224,128]{1,0:T(8,128)} %constant.17.clone.edge_h) | copy-start | bytes 344068
  9.7 0.9 %copy-start.10 = (f32[3,65,65]{2,1,0:T(8,128)S(1)}, f32[3,65,65]{2,1,0:T(8,128)}, u32[]{:S(2)}) copy-start(f32[3,65,65]{2,1,0:T(8,128)} %kern_real.1) | copy-start | bytes 152104
  10.6 0.9 %copy-start.11 = (f32[3,65,65]{2,1,0:T(8,128)S(1)}, f32[3,65,65]{2,1,0:T(8,128)}, u32[]{:S(2)}) copy-start(f32[3,65,65]{2,1,0:T(8,128)} %kern_imag.1) | copy-start | bytes 152104
  11.5 0.7 %copy-start.12 = (f32[3]{0:T(128)S(1)}, f32[3]{0:T(128)}, u32[]{:S(2)}) copy-start(f32[3]{0:T(128)} %weight.1) | copy-start | bytes 40
where the time goes:
time: 44.8 us; the launch traced here: 44.3 us
  Pallas kernels  31.5 us (70%)
  local copies, waits for them, and re-layouts  12.8 us (29%)
    pallas_call x1, Pallas kernels, body(): pl.pallas_call(kernel, out_shape=jax.ShapeDtypeStruct((BAND, 64), F32), i...  31.5 us
    unnamed x26, local copies, waits for them, and re-layouts  12.1 us

commit v1 on v0

--- a/solution.py
+++ b/solution.py
@@ -23,6 +23,8 @@
 NX = 224
 FX = NX // 2
 NY = 256
+RUN = 16
+PACK = 72 * OWN + 8
 FIELD = 160
 FROWS = 192
 
@@ -117,9 +119,20 @@
     mate = {"kern": 2 * half + (1 - core)}
     across = {"kern": 2 * (1 - half) + core}
 
+    place = lax.rem(tile, RUN)
+    head, tail = place == 0, place == RUN - 1
+    turn_before = head & (tile > 0)
+    turn_after = tail & (tile < tiles - 1)
+
     barrier = pltpu.get_barrier_semaphore()
-    for device in (before, after, across, mate):
+
+    def greet(device):
         pl.semaphore_signal(barrier, inc=1, device_id=device, device_id_type=MESH)
+
+    greet(across)
+    greet(mate)
+    pl.when(jnp.logical_not(tail))(lambda: greet(after))
+    pl.when(jnp.logical_not(head))(lambda: greet(before))
 
     pairs = (
         (kern_real, kr),
@@ -145,7 +158,6 @@
             src_ref=src, dst_ref=dst, send_sem=send_sem.at[index], recv_sem=recv_sem.at[index],
             device_id=device, device_id_type=MESH,
         )
-        copy.start()
         return copy
 
     for load in loads[:3]:
@@ -155,8 +167,8 @@
     for k in range(OWN):
         factor = jnp.sqrt(jnp.full((TAPS, TAPS), w[k], F32))
         real, imag = kr[k] * factor, ki[k] * factor
-        packed[k, 0:72, :] = jnp.zeros((72, 128), F32)
-        packed[k, 0:TAPS, :] = jnp.concatenate([real[:, 0:64], imag[:, 0:64]], axis=1)
+        packed[72 * k + 64 : 72 * k + 72, :] = jnp.zeros((8, 128), F32)
+        packed[72 * k : 72 * k + TAPS, :] = jnp.concatenate([real[:, 0:64], imag[:, 0:64]], axis=1)
         for grid in (real, imag):
             column = jnp.broadcast_to(grid[:, 64:65], (TAPS, 128))
             ends.append(jnp.sum(jnp.where(eye, column, 0.0), axis=0, keepdims=True))
@@ -164,17 +176,26 @@
     end_rows = jnp.zeros((8, 128), F32)
     for i, end in enumerate(ends):
         end_rows = jnp.where(row_id == i, jnp.broadcast_to(end, (8, 128)), end_rows)
-    packed[OWN, 0:72, :] = jnp.zeros((72, 128), F32)
-    packed[OWN, 0:8, :] = end_rows
-
-    pl.semaphore_wait(barrier, 4)
-    sends = [
-        send(0, packed.at[pl.ds(0, OWN + 1)], packed.at[pl.ds(OWN + 1, OWN + 1)], across),
-        send(1, logit.at[pl.ds(64, 64)], ext.at[pl.ds(0, 64)], after),
-        send(2, logit.at[pl.ds(0, 64)], ext.at[pl.ds(192, 64)], before),
-        send(3, target.at[pl.ds(96, RADIUS)], goal.at[pl.ds(0, RADIUS)], after),
-        send(4, target.at[pl.ds(0, RADIUS)], goal.at[pl.ds(160, RADIUS)], before),
-    ]
+    packed[72 * OWN : 72 * OWN + 8, :] = end_rows
+
+    ahead = jnp.where(tail, turn_after.astype(jnp.int32), 1)
+    pl.semaphore_wait(barrier, 2 + jnp.where(head, 0, 1) + ahead)
+    pl.when(turn_before)(lambda: greet(before))
+    pl.when(turn_after)(lambda: greet(after))
+
+    mask_down = send(0, logit.at[pl.ds(64, 64)], ext.at[pl.ds(0, 64)], after)
+    mask_up = send(1, logit.at[pl.ds(0, 64)], ext.at[pl.ds(192, 64)], before)
+    taps_over = send(2, packed.at[pl.ds(0, PACK)], packed.at[pl.ds(PACK, PACK)], across)
+    goal_down = send(3, target.at[pl.ds(96, RADIUS)], goal.at[pl.ds(0, RADIUS)], after)
+    goal_up = send(4, target.at[pl.ds(0, RADIUS)], goal.at[pl.ds(160, RADIUS)], before)
+    has_before, has_after = tile > 0, tile < tiles - 1
+    inner = jnp.logical_not(head)
+
+    pl.when(has_after)(mask_down.start)
+    pl.when(inner)(mask_up.start)
+    taps_over.start()
+    pl.when(has_after)(goal_down.start)
+    pl.when(inner)(goal_up.start)
 
     def butterfly(value):
         real0, real1 = value[:FX, :128], value[:FX, 128:]
@@ -184,11 +205,11 @@
         return even, odd
 
     def spectrum(group):
-        base = group * (OWN + 1)
-        ends = packed[base + OWN, 0:8, :]
+        base = group * PACK
+        ends = packed[base + 72 * OWN : base + PACK, :]
         edge = edge_c[...]
         for k in range(OWN):
-            taps = jnp.concatenate([packed[base + k], jnp.zeros((56, 128), F32)], 0)
+            taps = jnp.concatenate([packed[base + 72 * k : base + 72 * k + 72, :], jnp.zeros((56, 128), F32)], 0)
             half_way = left_mul((taps_c[0], taps_c[1]), taps, dot_t)
             stacked = []
             for part_id in range(2):
@@ -204,11 +225,20 @@
     for load in loads[3:6]:
         load.wait()
     spectrum(0)
+    taps_over.wait_recv()
+    spectrum(1)
 
     for load in loads[6:9]:
         load.wait()
-    sends[1].wait()
-    sends[2].wait()
+
+    @pl.when(turn_before)
+    def _():
+        pl.semaphore_wait(barrier, 1)
+        mask_up.start()
+        goal_up.start()
+
+    pl.when(has_before)(mask_down.wait_recv)
+    pl.when(has_after)(mask_up.wait_recv)
     row = lax.broadcasted_iota(jnp.int32, (NY, COLS), 0) - 64 + tile * BAND
     mask = jnp.where((row >= 0) & (row < tiles * BAND), jax.nn.sigmoid(3.0 * ext[...]), 0.0)
     even, odd = butterfly(left_mul((into_c[0], into_c[1]), mask, dot_t))
@@ -245,16 +275,14 @@
 
     inten = None
     for k in range(BOTH):
-        if k == OWN:
-            sends[0].wait()
-            spectrum(1)
         own = forward(k)
         inten = own if inten is None else inten + own
     part[...] = inten
     swap = send(5, part, part_in, mate)
-
-    sends[3].wait()
-    sends[4].wait()
+    swap.start()
+
+    pl.when(has_before)(goal_down.wait_recv)
+    pl.when(has_after)(goal_up.wait_recv)
     for load in loads[9:]:
         load.wait()
     goal_t = dot_t(pick_c[...], goal[...].astype(F32).astype(BF16))
@@ -264,8 +292,8 @@
     goal_t = jnp.concatenate([goal_t, jnp.zeros((FIELD, NY - FROWS), F32)], 1)
     slope = 12.0 * (printed - goal_t) * printed * (1.0 - printed)
     lane = lax.broadcasted_iota(jnp.int32, (FIELD, NY), 1)
-    place = lane - RADIUS + tile * BAND
-    slope = jnp.where((lane < FROWS) & (place >= 0) & (place < tiles * BAND), slope, 0.0)
+    line = lane - RADIUS + tile * BAND
+    slope = jnp.where((lane < FROWS) & (line >= 0) & (line < tiles * BAND), slope, 0.0)
 
     acc = [None, None]
     for k in range(BOTH):
@@ -295,18 +323,23 @@
     back = jnp.concatenate([back[:, :128], back[:, 128:]], 0)
     grad[...] = left_mul((last_c[0], last_c[1]), back, dot)
     swap_2 = send(6, grad.at[pl.ds(64, 64)], grad_in, mate)
-
-    own = jax.nn.sigmoid(3.0 * ext[64 : 64 + BAND, :])
-    own = jnp.where(half == 0, own[:, :128], own[:, 128:])
-    own = jnp.where(core == 0, own[:, :64], own[:, 64:])
+    swap_2.start()
+
+    own = ext[64 : 64 + BAND, :]
+    own = jnp.transpose(jnp.where(half == 0, own[:, :128], own[:, 128:]))
+    own = jax.nn.sigmoid(3.0 * jnp.where(core == 0, own[:64], own[64:]))
     factor = 3.0 * own * (1.0 - own)
     swap_2.wait()
-    total = grad[0:64, :] + grad_in[...]
-    result[...] = jnp.transpose(total) * factor
+    result[...] = (grad[0:64, :] + grad_in[...]) * factor
+    taps_over.wait_send()
+    for copy in (mask_down, goal_down):
+        pl.when(has_after)(copy.wait_send)
+    for copy in (mask_up, goal_up):
+        pl.when(has_before)(copy.wait_send)
 
 
 def body(consts, mask_logit, target, kern_real, kern_imag, kern_weight):
-    any_spec = pl.BlockSpec(memory_space=pl.ANY)
+    any_spec = pl.BlockSpec(memory_space=pltpu.HBM)
     vm = pltpu.VMEM
     scratch = [
         vm((NY, COLS), F32),
@@ -322,7 +355,7 @@
         vm((FIELD, COLS), BF16),
         vm((2, NX, FIELD), BF16),
         vm((2, 128, NX), BF16),
-        vm((2 * (OWN + 1), 72, 128), F32),
+        vm((2 * PACK, 128), F32),
         vm((BOTH, 2 * FX, 512), F32),
         vm((2 * BOTH, FIELD, NY), F32),
         vm((FIELD, NY), F32),
@@ -333,16 +366,17 @@
         pltpu.SemaphoreType.DMA((7,)),
         pltpu.SemaphoreType.DMA((7,)),
     ]
-    return pl.pallas_call(
+    total = pl.pallas_call(
         kernel,
-        out_shape=jax.ShapeDtypeStruct((BAND, 64), F32),
+        out_shape=pltpu.VMEM((64, BAND), F32),
         in_specs=[any_spec] * (5 + len(NAMES)),
         out_specs=pl.BlockSpec(memory_space=pltpu.VMEM),
         scratch_shapes=scratch,
         compiler_params=pltpu.CompilerParams(
             collective_id=0, has_side_effects=True, vmem_limit_bytes=48 * 2**20
         ),
-    )(mask_logit, target, kern_real, kern_imag, kern_weight, *consts)
+    )(*[pltpu.with_memory_space_constraint(v, pltpu.HBM) for v in (mask_logit, target, kern_real, kern_imag, kern_weight, *consts)])
+    return total.T
 
 
 def solution(mesh):

time: 44.8 us -> 26.9 us (0.60)
  the two profiles are of different devices: /device:TPU:1 before, /device:TPU:7 now
where the time goes in v1:
time: 26.9 us; the launch traced here: 26.8 us
  Pallas kernels  26.2 us (97%)
  local copies, waits for them, and re-layouts  0.62 us (2%)
    pallas_call x1, Pallas kernels, body(): pl.pallas_call(kernel, out_shape=pltpu.VMEM((64, BAND), F32), in_specs=[a...  26.2 us
    unnamed x1, local copies, waits for them, and re-layouts  0.62 us

profile of v1, /device:TPU:7, one launch (start us, length us, event | category | flops | bytes accessed | tf_op | source)
XLA Modules:
  0.0 26.8 jit_solution(12176941339341463399)
XLA Ops:
  0.0 26.2 %shard_map.127 = f32[64,128]{1,0:T(8,128)S(1)} custom-call(f32[128,256]{1,0:T(8,128)} %logit.1, s32[128,256]{1,0:T(8,128)} %target.1, f32[3,65,65]{2,1,0:T(8,128)} %kern_real.1, f32[3,65,65]{2,1,0:T(8,128)} %kern_imag.1, f32[3]{0:T(128)} %weight.1, bf16[2,448,128]{2,1,0:T(8,128)(2,1)} %constant.16.clone.taps_h, f32[224,128]{1,0:T(8,128)} %constant.17.clone.edge_h, ...), custom_call_target="tpu_custom_call" | custom-call | tf_op jit(solution)/shard_map/pallas_call | solution.py:369
  26.2 0.6 %copy.15 = f32[128,64]{0,1:T(8,128)} copy(f32[128,64]{0,1:T(8,128)S(1)} %bitcast.1) | data formatting | bytes 65536

commit v2 on v1

--- a/solution.py
+++ b/solution.py
@@ -109,7 +109,7 @@
     result,
     ext, goal, kr, ki, w, taps_c, edge_c, rows_c, into_c, out_c, pick_c, back_c, last_c,
     packed, spec, fields, part, part_in, grad, grad_in,
-    local_sem, send_sem, recv_sem,
+    local_sem, send_sem, recv_sem, relay,
 ):
     tile, kern = lax.axis_index("tile"), lax.axis_index("kern")
     tiles = lax.axis_size("tile")
@@ -121,6 +121,7 @@
 
     place = lax.rem(tile, RUN)
     head, tail = place == 0, place == RUN - 1
+    eve = place == RUN - 2
     turn_before = head & (tile > 0)
     turn_after = tail & (tile < tiles - 1)
 
@@ -129,10 +130,15 @@
     def greet(device):
         pl.semaphore_signal(barrier, inc=1, device_id=device, device_id_type=MESH)
 
-    greet(across)
-    greet(mate)
-    pl.when(jnp.logical_not(tail))(lambda: greet(after))
-    pl.when(jnp.logical_not(head))(lambda: greet(before))
+    inner = jnp.logical_not(tail)
+
+    @pl.when(inner)
+    def _():
+        greet(across)
+        greet(mate)
+
+    pl.when(inner & jnp.logical_not(eve))(lambda: greet(after))
+    pl.when(inner & jnp.logical_not(head))(lambda: greet(before))
 
     pairs = (
         (kern_real, kr),
@@ -149,16 +155,31 @@
         (back_h.at[half], back_c),
         (last_h.at[kern], last_c),
     )
+    def send(index, src, dst, device):
+        return pltpu.make_async_remote_copy(
+            src_ref=src, dst_ref=dst, send_sem=send_sem.at[index], recv_sem=recv_sem.at[index],
+            device_id=device, device_id_type=MESH,
+        )
+
+    mask_down = send(0, logit.at[pl.ds(64, 64)], ext.at[pl.ds(0, 64)], after)
+    mask_up = send(1, logit.at[pl.ds(0, 64)], ext.at[pl.ds(192, 64)], before)
+    taps_over = send(2, packed.at[pl.ds(0, PACK)], packed.at[pl.ds(PACK, PACK)], across)
+    goal_down = send(3, target.at[pl.ds(96, RADIUS)], goal.at[pl.ds(0, RADIUS)], after)
+    goal_up = send(4, target.at[pl.ds(0, RADIUS)], goal.at[pl.ds(160, RADIUS)], before)
+    has_before, has_after = tile > 0, tile < tiles - 1
+
+    @pl.when(turn_after)
+    def _():
+        pl.semaphore_wait(barrier, 1)
+        mask_down.start()
+        goal_down.start()
+        greet(after)
+
+    pl.when(tail)(lambda: greet(before))
+
     loads = [pltpu.make_async_copy(src, dst, local_sem.at[i]) for i, (src, dst) in enumerate(pairs)]
     for load in loads:
         load.start()
-
-    def send(index, src, dst, device):
-        copy = pltpu.make_async_remote_copy(
-            src_ref=src, dst_ref=dst, send_sem=send_sem.at[index], recv_sem=recv_sem.at[index],
-            device_id=device, device_id_type=MESH,
-        )
-        return copy
 
     for load in loads[:3]:
         load.wait()
@@ -178,24 +199,22 @@
         end_rows = jnp.where(row_id == i, jnp.broadcast_to(end, (8, 128)), end_rows)
     packed[72 * OWN : 72 * OWN + 8, :] = end_rows
 
-    ahead = jnp.where(tail, turn_after.astype(jnp.int32), 1)
-    pl.semaphore_wait(barrier, 2 + jnp.where(head, 0, 1) + ahead)
-    pl.when(turn_before)(lambda: greet(before))
-    pl.when(turn_after)(lambda: greet(after))
-
-    mask_down = send(0, logit.at[pl.ds(64, 64)], ext.at[pl.ds(0, 64)], after)
-    mask_up = send(1, logit.at[pl.ds(0, 64)], ext.at[pl.ds(192, 64)], before)
-    taps_over = send(2, packed.at[pl.ds(0, PACK)], packed.at[pl.ds(PACK, PACK)], across)
-    goal_down = send(3, target.at[pl.ds(96, RADIUS)], goal.at[pl.ds(0, RADIUS)], after)
-    goal_up = send(4, target.at[pl.ds(0, RADIUS)], goal.at[pl.ds(160, RADIUS)], before)
-    has_before, has_after = tile > 0, tile < tiles - 1
-    inner = jnp.logical_not(head)
-
-    pl.when(has_after)(mask_down.start)
-    pl.when(inner)(mask_up.start)
-    taps_over.start()
-    pl.when(has_after)(goal_down.start)
-    pl.when(inner)(goal_up.start)
+    @pl.when(inner)
+    def _():
+        pl.semaphore_wait(barrier, 3 + jnp.where(head, 0, 1))
+        pl.when(turn_before)(lambda: greet(before))
+        mask_down.start()
+        pl.when(jnp.logical_not(head))(mask_up.start)
+        taps_over.start()
+        goal_down.start()
+        pl.when(jnp.logical_not(head))(goal_up.start)
+
+    @pl.when(eve)
+    def _():
+        for device in (across, mate):
+            pl.semaphore_signal(relay, inc=1, device_id=device, device_id_type=MESH)
+        pl.semaphore_wait(relay, 2)
+        greet(after)
 
     def butterfly(value):
         real0, real1 = value[:FX, :128], value[:FX, 128:]
@@ -225,6 +244,14 @@
     for load in loads[3:6]:
         load.wait()
     spectrum(0)
+
+    @pl.when(tail)
+    def _():
+        pl.semaphore_wait(barrier, 1)
+        mask_up.start()
+        taps_over.start()
+        goal_up.start()
+
     taps_over.wait_recv()
     spectrum(1)
 
@@ -365,6 +392,7 @@
         pltpu.SemaphoreType.DMA((13,)),
         pltpu.SemaphoreType.DMA((7,)),
         pltpu.SemaphoreType.DMA((7,)),
+        pltpu.SemaphoreType.REGULAR,
     ]
     total = pl.pallas_call(
         kernel,

time: 26.9 us -> 25.4 us (0.944)
  the two profiles are of different devices: /device:TPU:7 before, /device:TPU:1 now
where the time goes in v2:
time: 25.4 us; the launch traced here: 25.3 us
  Pallas kernels  24.7 us (97%)
  local copies, waits for them, and re-layouts  0.62 us (2%)
    pallas_call x1, Pallas kernels, body(): pl.pallas_call(kernel, out_shape=pltpu.VMEM((64, BAND), F32), in_specs=[a...  24.7 us
    unnamed x1, local copies, waits for them, and re-layouts  0.62 us

profile of v2, /device:TPU:1, one launch (start us, length us, event | category | flops | bytes accessed | tf_op | source)
XLA Modules:
  0.0 25.3 jit_solution(16444283970584870030)
XLA Ops:
  0.0 24.7 %shard_map.127 = f32[64,128]{1,0:T(8,128)S(1)} custom-call(f32[128,256]{1,0:T(8,128)} %logit.1, s32[128,256]{1,0:T(8,128)} %target.1, f32[3,65,65]{2,1,0:T(8,128)} %kern_real.1, f32[3,65,65]{2,1,0:T(8,128)} %kern_imag.1, f32[3]{0:T(128)} %weight.1, bf16[2,448,128]{2,1,0:T(8,128)(2,1)} %constant.16.clone.taps_h, f32[224,128]{1,0:T(8,128)} %constant.17.clone.edge_h, ...), custom_call_target="tpu_custom_call" | custom-call | tf_op jit(solution)/shard_map/pallas_call | solution.py:397
  24.7 0.6 %copy.15 = f32[128,64]{0,1:T(8,128)} copy(f32[128,64]{0,1:T(8,128)S(1)} %bitcast.1) | data formatting | bytes 65536

commit v3 on v2

--- a/solution.py
+++ b/solution.py
@@ -29,10 +29,14 @@
 FROWS = 192
 
 
-def pair(table):
+def triple(table, axis, order):
     high = table.astype(ml_dtypes.bfloat16)
     low = (table - high.astype(np.float64)).astype(ml_dtypes.bfloat16)
-    return np.stack([high, low])
+    return np.concatenate([(high, low)[i] for i in order], axis)
+
+
+LEFT = (0, 1, 0)
+RIGHT = (0, 0, 1)
 
 
 def tables():
@@ -47,27 +51,30 @@
     for half in range(2):
         local = np.arange(COLS) - 64 * half
         full = wave(local) * ((local >= 0) & (local < 192))[None, :]
-        into.append(pair(full))
+        into.append(triple(full, 1, LEFT))
         part = full[:, 96 * half : 96 * half + FIELD]
-        back_in.append(pair(part))
-        out.append(pair(scale * part.T))
+        back_in.append(triple(part, 1, LEFT))
+        out.append(triple(scale * part.T, 1, LEFT))
         for core in range(2):
             cols = np.concatenate([64 * (2 * half + c) + np.arange(64) for c in (core, 1 - core)])
-            last.append(pair(2.0 * scale * full[:, cols].T))
+            last.append(triple(2.0 * scale * full[:, cols].T, 1, LEFT))
         pick.append((np.arange(COLS)[None, :] == np.arange(FIELD)[:, None] + 96 * half))
     taps = wave(np.arange(64) - RADIUS)
     zero = np.zeros_like(taps)
     taps = np.concatenate([np.concatenate([taps, zero], 1), np.concatenate([zero, taps], 1)], 0)
     edge = np.broadcast_to(wave(np.array([RADIUS])), (NX, 128))
-    rows = []
+    rows, rows_t = [], []
     for odd in range(2):
         angle = 2.0 * np.pi * np.arange(128)[:, None] * (2 * np.arange(128) + odd)[None, :] / NY
         c, s = np.cos(angle), np.sin(angle)
-        rows.append(pair(np.concatenate([np.concatenate([c, -s], 1), np.concatenate([s, c], 1)], 0)))
+        table = np.concatenate([np.concatenate([c, -s], 1), np.concatenate([s, c], 1)], 0)
+        rows.append(triple(table, 0, RIGHT))
+        rows_t.append(triple(table.T, 0, RIGHT))
     return dict(
         rows=np.stack(rows),
+        rows_t=np.stack(rows_t),
         into=np.stack(into),
-        taps=pair(taps),
+        taps=triple(taps, 1, LEFT),
         edge=edge.astype(np.float32),
         out=np.stack(out),
         back_in=np.stack(back_in),
@@ -76,7 +83,7 @@
     )
 
 
-NAMES = ("taps", "edge", "rows", "into", "out", "pick", "back_in", "last")
+NAMES = ("taps", "edge", "rows", "rows_t", "into", "out", "pick", "back_in", "last")
 
 
 def split(value):
@@ -92,23 +99,29 @@
     return lax.dot_general(left, right, (((1,), (1,)), ((), ())), preferred_element_type=F32)
 
 
-def right_mul(value, table, mul):
+def spread(value):
     high, low = split(value)
-    count = value.shape[0]
-    both = mul(jnp.concatenate([high, low], 0), table[0])
-    return both[:count] + both[count:] + mul(high, table[1])
-
-
-def left_mul(table, value, mul):
+    return jnp.concatenate([high, low, high], 1)
+
+
+def right_mul(value, table):
+    return dot(spread(value), table)
+
+
+def heap(value, axis=0):
     high, low = split(value)
-    return mul(table[0], high) + mul(table[1], high) + mul(table[0], low)
+    return jnp.concatenate([high, high, low], axis)
+
+
+def left_mul(table, value, mul=dot):
+    return mul(table, heap(value, 1 if mul is dot_t else 0))
 
 
 def kernel(
-    logit, target, kern_real, kern_imag, weight, taps_h, edge_h, rows_h, into_h, out_h, pick_h, back_h, last_h,
+    logit, target, kern_real, kern_imag, weight, taps_h, edge_h, rows_h, rows_t_h, into_h, out_h, pick_h, back_h, last_h,
     result,
-    ext, goal, kr, ki, w, taps_c, edge_c, rows_c, into_c, out_c, pick_c, back_c, last_c,
-    packed, spec, fields, part, part_in, grad, grad_in,
+    ext, goal, kr, ki, w, taps_c, edge_c, rows_c, rows_t_c, into_c, out_c, pick_c, back_c, last_c,
+    packed, spec, streams, waves, near, far, packs, begun, ended, part, part_in, grad, grad_in,
     local_sem, send_sem, recv_sem, relay,
 ):
     tile, kern = lax.axis_index("tile"), lax.axis_index("kern")
@@ -147,6 +160,7 @@
         (taps_h, taps_c),
         (edge_h, edge_c),
         (rows_h, rows_c),
+        (rows_t_h, rows_t_c),
         (logit, ext.at[pl.ds(64, BAND)]),
         (into_h.at[half], into_c),
         (out_h.at[half], out_c),
@@ -229,17 +243,14 @@
         edge = edge_c[...]
         for k in range(OWN):
             taps = jnp.concatenate([packed[base + 72 * k : base + 72 * k + 72, :], jnp.zeros((56, 128), F32)], 0)
-            half_way = left_mul((taps_c[0], taps_c[1]), taps, dot_t)
-            stacked = []
-            for part_id in range(2):
-                row = ends[2 * k + part_id : 2 * k + part_id + 1, :]
-                own = half_way[NX * part_id : NX * (part_id + 1)] + edge * row
-                stacked.append(jnp.concatenate([own[:FX], own[FX:]], 1))
-            value = jnp.concatenate(stacked, 0)
-            for odd in range(2):
-                spec[group * OWN + k, :, 256 * odd : 256 * odd + 256] = right_mul(
-                    value, (rows_c[odd, 0], rows_c[odd, 1]), dot
-                )
+            half_way = left_mul(taps_c[...], taps, dot_t)
+            for c in range(2):
+                row = ends[2 * k + c : 2 * k + c + 1, :]
+                own = half_way[NX * c : NX * (c + 1)] + edge * row
+                streams[0, k, FX * c : FX * (c + 1), :] = spread(jnp.concatenate([own[:FX], own[FX:]], 1))
+        for odd in range(2):
+            for k in range(OWN):
+                spec[group * OWN + k, :, 256 * odd : 256 * odd + 256] = dot(streams[0, k], rows_c[odd])
 
     for load in loads[3:6]:
         load.wait()
@@ -255,7 +266,7 @@
     taps_over.wait_recv()
     spectrum(1)
 
-    for load in loads[6:9]:
+    for load in loads[6:10]:
         load.wait()
 
     @pl.when(turn_before)
@@ -268,70 +279,90 @@
     pl.when(has_after)(mask_up.wait_recv)
     row = lax.broadcasted_iota(jnp.int32, (NY, COLS), 0) - 64 + tile * BAND
     mask = jnp.where((row >= 0) & (row < tiles * BAND), jax.nn.sigmoid(3.0 * ext[...]), 0.0)
-    even, odd = butterfly(left_mul((into_c[0], into_c[1]), mask, dot_t))
+    even, odd = butterfly(left_mul(into_c[...], mask, dot_t))
     mask_spec = (
-        right_mul(even, (rows_c[0, 0], rows_c[0, 1]), dot),
-        right_mul(odd, (rows_c[1, 0], rows_c[1, 1]), dot),
+        right_mul(even, rows_c[0]),
+        right_mul(odd, rows_c[1]),
     )
 
-    def forward(k):
-        ends = []
+    first_half = lax.broadcasted_iota(jnp.int32, (1, 128), 1) < 64
+
+    def halves(left, right):
+        return jnp.where(first_half, left, pltpu.roll(right, 64, 1))
+
+    def square(field):
+        return field[:, :128] * field[:, :128] + field[:, 128:] * field[:, 128:]
+
+    total, tails = None, []
+    for k in range(BOTH):
         for odd in range(2):
             mr, mi = mask_spec[odd][:, :128], mask_spec[odd][:, 128:]
-            rows = []
             for c in range(2):
                 sr = spec[k, FX * c : FX * (c + 1), 256 * odd : 256 * odd + 128]
                 si = spec[k, FX * c : FX * (c + 1), 256 * odd + 128 : 256 * odd + 256]
-                rows.append(jnp.concatenate([sr * mr + si * mi, sr * mi - si * mr], 1))
-            ends.append(right_mul(jnp.concatenate(rows, 0), (rows_c[odd, 0], rows_c[odd, 1]), dot_t))
+                streams[odd, k, FX * c : FX * (c + 1), :] = spread(
+                    jnp.concatenate([sr * mr + si * mi, sr * mi - si * mr], 1)
+                )
+    for k in range(BOTH):
+        ends = [dot(streams[odd, k], rows_t_c[odd]) for odd in range(2)]
         plus, minus = ends[0] + ends[1], ends[0] - ends[1]
-        total = None
-        for c in range(2):
-            rows = slice(FX * c, FX * (c + 1))
-            wave = jnp.concatenate(
-                [
-                    jnp.concatenate([plus[rows, :128], minus[rows, :128]], 1),
-                    jnp.concatenate([plus[rows, 128:], minus[rows, 128:]], 1),
-                ],
-                0,
-            )
-            field = left_mul((out_c[0], out_c[1]), wave, dot)
-            fields[2 * k + c] = field
-            total = field * field if total is None else total + field * field
-        return total
-
-    inten = None
-    for k in range(BOTH):
-        own = forward(k)
-        inten = own if inten is None else inten + own
-    part[...] = inten
-    swap = send(5, part, part_in, mate)
-    swap.start()
+        plus_c = [jnp.concatenate([plus[FX * c : FX * (c + 1), :128], plus[FX * c : FX * (c + 1), 128:]], 0) for c in (0, 1)]
+        minus_c = [jnp.concatenate([minus[FX * c : FX * (c + 1), :128], minus[FX * c : FX * (c + 1), 128:]], 0) for c in (0, 1)]
+        waves[k] = heap(jnp.concatenate(plus_c, 1))
+        packs[k] = halves(*minus_c)
+    for k in range(BOTH):
+        field = dot(out_c[...], waves[k])
+        near[k] = field
+        total = square(field) if total is None else total + square(field)
+    part[0] = total
+    swap_near = send(5, part.at[0], part_in.at[0], mate)
+    swap_near.start()
+    total = None
+    for k in range(BOTH // 2):
+        field = left_mul(out_c[...], jnp.concatenate([packs[2 * k], packs[2 * k + 1]], 1), dot)
+        far[k] = field
+        total = square(field) if total is None else total + square(field)
+    part[1] = total + pltpu.roll(total, 64, 1)
+    swap_far = send(7, part.at[1], part_in.at[1], mate)
+    swap_far.start()
 
     pl.when(has_before)(goal_down.wait_recv)
     pl.when(has_after)(goal_up.wait_recv)
-    for load in loads[9:]:
+    for load in loads[10:]:
         load.wait()
     goal_t = dot_t(pick_c[...], goal[...].astype(F32).astype(BF16))
-
-    swap.wait()
-    printed = jax.nn.sigmoid(6.0 * (part[...] + part_in[...] - 1.0))
-    goal_t = jnp.concatenate([goal_t, jnp.zeros((FIELD, NY - FROWS), F32)], 1)
-    slope = 12.0 * (printed - goal_t) * printed * (1.0 - printed)
-    lane = lax.broadcasted_iota(jnp.int32, (FIELD, NY), 1)
-    line = lane - RADIUS + tile * BAND
-    slope = jnp.where((lane < FROWS) & (line >= 0) & (line < tiles * BAND), slope, 0.0)
-
+    goal_far = goal_t[:, 128:]
+    goal_far = jnp.concatenate([goal_far, goal_far], 1)
+
+    lane = lax.broadcasted_iota(jnp.int32, (FIELD, 128), 1)
+
+    def slope_of(which, goal_part, start):
+        printed = jax.nn.sigmoid(6.0 * (part[which] + part_in[which] - 1.0))
+        slope = 12.0 * (printed - goal_part) * printed * (1.0 - printed)
+        line = start - RADIUS + tile * BAND
+        slope = jnp.where((line >= 0) & (line < tiles * BAND), slope, 0.0)
+        return jnp.concatenate([slope, slope], 1)
+
+    swap_near.wait()
+    slope = slope_of(0, goal_t[:, :128], lane)
+    for k in range(BOTH):
+        begun[k] = left_mul(back_c[...], slope * near[k])
+    swap_far.wait()
+    slope = slope_of(1, goal_far, 128 + lax.rem(lane, 64))
+    for k in range(BOTH // 2):
+        ended[k] = left_mul(back_c[...], slope * far[k])
     acc = [None, None]
     for k in range(BOTH):
-        evens, odds = [], []
+        own = ended[k // 2, :, 128 * (k % 2) : 128 * (k % 2) + 128]
+        low_rows = [jnp.where(first_half, own, 0.0), jnp.where(first_half, pltpu.roll(own, 64, 1), 0.0)]
         for c in range(2):
-            source = slope * fields[2 * k + c]
-            even, odd = butterfly(left_mul((back_c[0], back_c[1]), source, dot))
-            evens.append(even)
-            odds.append(odd)
-        for odd, values in enumerate((evens, odds)):
-            wave = right_mul(jnp.concatenate(values, 0), (rows_c[odd, 0], rows_c[odd, 1]), dot)
+            head_rows = begun[k, :, 128 * c : 128 * c + 128]
+            even, odd = head_rows + low_rows[c], head_rows - low_rows[c]
+            streams[0, k, FX * c : FX * (c + 1), :] = spread(jnp.concatenate([even[:FX], even[FX:]], 1))
+            streams[1, k, FX * c : FX * (c + 1), :] = spread(jnp.concatenate([odd[:FX], odd[FX:]], 1))
+    for k in range(BOTH):
+        for odd in range(2):
+            wave = dot(streams[odd, k], rows_c[odd])
             for c in range(2):
                 rows = slice(FX * c, FX * (c + 1))
                 sr = spec[k, FX * c : FX * (c + 1), 256 * odd : 256 * odd + 128]
@@ -346,9 +377,9 @@
     sign = 1.0 - 2.0 * lax.rem(lax.broadcasted_iota(jnp.int32, (FX, 128), 1), 2).astype(F32)
     even = jnp.concatenate([acc[0][0] * sign, acc[0][1] * sign], 1)
     odd = jnp.concatenate([-acc[1][1] * sign, acc[1][0] * sign], 1)
-    back = right_mul(even, (rows_c[0, 0], rows_c[0, 1]), dot_t) + right_mul(odd, (rows_c[1, 0], rows_c[1, 1]), dot_t)
+    back = right_mul(even, rows_t_c[0]) + right_mul(odd, rows_t_c[1])
     back = jnp.concatenate([back[:, :128], back[:, 128:]], 0)
-    grad[...] = left_mul((last_c[0], last_c[1]), back, dot)
+    grad[...] = left_mul(last_c[...], back, dot)
     swap_2 = send(6, grad.at[pl.ds(64, 64)], grad_in, mate)
     swap_2.start()
 
@@ -374,24 +405,31 @@
         vm((OWN, TAPS, TAPS), F32),
         vm((OWN, TAPS, TAPS), F32),
         pltpu.SMEM((OWN,), F32),
-        vm((2, 2 * NX, 128), BF16),
+        vm((2 * NX, 3 * 128), BF16),
         vm((NX, 128), F32),
-        vm((2, 2, 256, 256), BF16),
-        vm((2, NX, COLS), BF16),
-        vm((2, FIELD, NX), BF16),
+        vm((2, 768, 256), BF16),
+        vm((2, 768, 256), BF16),
+        vm((NX, 3 * COLS), BF16),
+        vm((FIELD, 3 * NX), BF16),
         vm((FIELD, COLS), BF16),
-        vm((2, NX, FIELD), BF16),
-        vm((2, 128, NX), BF16),
+        vm((NX, 3 * FIELD), BF16),
+        vm((128, 3 * NX), BF16),
         vm((2 * PACK, 128), F32),
         vm((BOTH, 2 * FX, 512), F32),
-        vm((2 * BOTH, FIELD, NY), F32),
-        vm((FIELD, NY), F32),
-        vm((FIELD, NY), F32),
+        vm((2, BOTH, 2 * FX, 768), BF16),
+        vm((BOTH, 3 * NX, 256), BF16),
+        vm((BOTH, FIELD, 256), F32),
+        vm((BOTH // 2, FIELD, 256), F32),
+        vm((BOTH, 2 * FX, 128), F32),
+        vm((BOTH, 2 * FX, 256), F32),
+        vm((BOTH // 2, 2 * FX, 256), F32),
+        vm((2, FIELD, 128), F32),
+        vm((2, FIELD, 128), F32),
         vm((128, BAND), F32),
         vm((64, BAND), F32),
-        pltpu.SemaphoreType.DMA((13,)),
-        pltpu.SemaphoreType.DMA((7,)),
-        pltpu.SemaphoreType.DMA((7,)),
+        pltpu.SemaphoreType.DMA((14,)),
+        pltpu.SemaphoreType.DMA((8,)),
+        pltpu.SemaphoreType.DMA((8,)),
         pltpu.SemaphoreType.REGULAR,
     ]
     total = pl.pallas_call(

time: 25.4 us -> 22.9 us (0.902)
  Pallas kernels: 24.7 us -> 22.1 us
    pallas_call x1, Pallas kernels: 24.7 us -> 22.1 us  [body(): pl.pallas_call(kernel, out_shape=pltpu.VMEM((64, BAND), F32), in_specs=[a...]
where the time goes in v3:
time: 22.9 us; the launch traced here: 22.8 us
  Pallas kernels  22.1 us (97%)
  local copies, waits for them, and re-layouts  0.62 us (3%)
    pallas_call x1, Pallas kernels, body(): pl.pallas_call(kernel, out_shape=pltpu.VMEM((64, BAND), F32), in_specs=[a...  22.1 us
    unnamed x1, local copies, waits for them, and re-layouts  0.62 us

profile of v3, /device:TPU:1, one launch (start us, length us, event | category | flops | bytes accessed | tf_op | source)
XLA Modules:
  0.0 22.8 jit_solution(18410074868837327606)
XLA Ops:
  0.0 22.1 %shard_map.136 = f32[64,128]{1,0:T(8,128)S(1)} custom-call(f32[128,256]{1,0:T(8,128)} %logit.1, s32[128,256]{1,0:T(8,128)} %target.1, f32[3,65,65]{2,1,0:T(8,128)} %kern_real.1, f32[3,65,65]{2,1,0:T(8,128)} %kern_imag.1, f32[3]{0:T(128)} %weight.1, bf16[448,384]{1,0:T(8,128)(2,1)} %constant.18.clone.taps_h, f32[224,128]{1,0:T(8,128)} %constant.19.clone.edge_h, ...), custom_call_target="tpu_custom_call" | custom-call | tf_op jit(solution)/shard_map/pallas_call | solution.py:435
  22.1 0.6 %copy.16 = f32[128,64]{0,1:T(8,128)} copy(f32[128,64]{0,1:T(8,128)S(1)} %bitcast.1) | data formatting | bytes 65536

commit v4 on v3

v4 whole, which is shorter than its diff:
```python
import functools
import math

import jax
import jax.numpy as jnp
import ml_dtypes
import numpy as np
from jax import lax
from jax.experimental import pallas as pl
from jax.experimental.pallas import tpu as pltpu
from jax.sharding import PartitionSpec as P

F32 = jnp.float32
BF16 = jnp.bfloat16
MESH = pl.DeviceIdType.MESH

BAND = 128
COLS = 256
TAPS = 65
RADIUS = 32
OWN = 3
BOTH = 2 * OWN
NX = 224
FX = NX // 2
NY = 128
RUN = 16
PACK = 72 * OWN + 8
FIELD = 160
FROWS = 192


def triple(table, axis, order):
    high = table.astype(ml_dtypes.bfloat16)
    low = (table - high.astype(np.float64)).astype(ml_dtypes.bfloat16)
    return np.concatenate([(high, low)[i] for i in order], axis)


LEFT = (0, 1, 0)
RIGHT = (0, 0, 1)


def tables():
    theta = 2.0 * np.pi * (np.arange(FX) + 0.5) / NX

    def wave(offsets):
        angle = theta[:, None] * offsets[None, :]
        return np.concatenate([np.cos(angle), -np.sin(angle)], 0)

    scale = 2.0 / (NX * NY)
    into, back_in, out, last, pick = [], [], [], [], []
    for half in range(2):
        local = np.arange(COLS) - 64 * half
        full = wave(local) * ((local >= 0) & (local < 192))[None, :]
        into.append(triple(full, 1, LEFT))
        part = full[:, 96 * half : 96 * half + FIELD]
        back_in.append(triple(part, 1, LEFT))
        out.append(triple(scale * part.T, 1, LEFT))
        for core in range(2):
            cols = np.concatenate([64 * (2 * half + c) + np.arange(64) for c in (core, 1 - core)])
            last.append(triple(2.0 * scale * full[:, cols].T, 1, LEFT))
        pick.append((np.arange(COLS)[None, :] == np.arange(FIELD)[:, None] + 96 * half))
    taps = wave(np.arange(64) - RADIUS)
    zero = np.zeros_like(taps)
    taps = np.concatenate([np.concatenate([taps, zero], 1), np.concatenate([zero, taps], 1)], 0)
    edge = np.broadcast_to(wave(np.array([RADIUS])), (NX, 128))
    angle = 2.0 * np.pi * np.arange(NY)[:, None] * np.arange(NY)[None, :] / NY
    c, s = np.cos(angle), np.sin(angle)
    rows = np.concatenate([np.concatenate([c, -s], 1), np.concatenate([s, c], 1)], 0)
    return dict(
        rows=triple(rows, 0, RIGHT),
        rows_t=triple(rows.T, 0, RIGHT),
        into=np.stack(into),
        taps=triple(taps, 1, LEFT),
        edge=edge.astype(np.float32),
        out=np.stack(out),
        back_in=np.stack(back_in),
        last=np.stack(last),
        pick=np.stack(pick).astype(ml_dtypes.bfloat16),
    )


NAMES = ("taps", "edge", "rows", "rows_t", "into", "out", "pick", "back_in", "last")


def split(value):
    high = value.astype(BF16)
    return high, (value - high.astype(F32)).astype(BF16)


def dot(left, right):
    return jnp.dot(left, right, preferred_element_type=F32)


def dot_t(left, right):
    return lax.dot_general(left, right, (((1,), (1,)), ((), ())), preferred_element_type=F32)


def spread(value):
    high, low = split(value)
    return jnp.concatenate([high, low, high], 1)


def right_mul(value, table):
    return dot(spread(value), table)


def heap(value, axis=0):
    high, low = split(value)
    return jnp.concatenate([high, high, low], axis)


def left_mul(table, value, mul=dot):
    return mul(table, heap(value, 1 if mul is dot_t else 0))


def kernel(
    logit, target, kern_real, kern_imag, weight, taps_h, edge_h, rows_h, rows_t_h, into_h, out_h, pick_h, back_h, last_h,
    result,
    ext, goal, kr, ki, w, taps_c, edge_c, rows_c, rows_t_c, into_c, out_c, pick_c, back_c, last_c,
    packed, spec, columns, middle, lower, held, streams, waves, near, far, packs, begun, ended, part, part_in, grad, grad_in,
    local_sem, send_sem, recv_sem, relay,
):
    tile, kern = lax.axis_index("tile"), lax.axis_index("kern")
    tiles = lax.axis_size("tile")
    half, core = kern // 2, lax.rem(kern, 2)
    before = {"tile": lax.rem(tile + tiles - 1, tiles)}
    after = {"tile": lax.rem(tile + 1, tiles)}
    mate = {"kern": 2 * half + (1 - core)}
    across = {"kern": 2 * (1 - half) + core}
    beyond = {"tile": lax.rem(tile + tiles - 1, tiles), "kern": 2 * (1 - half) + core}
    onward = {"tile": lax.rem(tile + 1, tiles), "kern": 2 * (1 - half) + core}

    place = lax.rem(tile, RUN)
    head, tail = place == 0, place == RUN - 1
    eve = place == RUN - 2
    turn_before = head & (tile > 0)
    turn_after = tail & (tile < tiles - 1)

    barrier = pltpu.get_barrier_semaphore()

    def greet(device):
        pl.semaphore_signal(barrier, inc=1, device_id=device, device_id_type=MESH)

    inner = jnp.logical_not(tail)

    @pl.when(inner)
    def _():
        greet(across)
        greet(mate)

    pl.when(inner & jnp.logical_not(eve))(lambda: greet(after))
    pl.when(inner & jnp.logical_not(head))(lambda: greet(before))

    pairs = (
        (kern_real, kr),
        (kern_imag, ki),
        (weight, w),
        (taps_h, taps_c),
        (edge_h, edge_c),
        (rows_h, rows_c),
        (rows_t_h, rows_t_c),
        (logit, ext.at[pl.ds(64, BAND)]),
        (into_h.at[half], into_c),
        (out_h.at[half], out_c),
        (target, goal.at[pl.ds(RADIUS, BAND)]),
        (pick_h.at[half], pick_c),
        (back_h.at[half], back_c),
        (last_h.at[kern], last_c),
    )
    def send(index, src, dst, device, arrival=None):
        arrival = index if arrival is None else arrival
        return pltpu.make_async_remote_copy(
            src_ref=src, dst_ref=dst, send_sem=send_sem.at[index], recv_sem=recv_sem.at[arrival],
            device_id=device, device_id_type=MESH,
        )

    mask_down = send(0, logit.at[pl.ds(64, 64)], ext.at[pl.ds(0, 64)], after)
    mask_up = send(1, logit.at[pl.ds(0, 64)], ext.at[pl.ds(192, 64)], before)
    taps_over = send(2, packed.at[pl.ds(0, PACK)], packed.at[pl.ds(PACK, PACK)], across)
    taps_on = send(8, packed.at[pl.ds(0, PACK)], packed.at[pl.ds(PACK, PACK)], onward, 2)
    goal_down = send(3, target.at[pl.ds(96, RADIUS)], goal.at[pl.ds(0, RADIUS)], after)
    goal_up = send(4, target.at[pl.ds(0, RADIUS)], goal.at[pl.ds(160, RADIUS)], before)
    has_before, has_after = tile > 0, tile < tiles - 1

    @pl.when(turn_after)
    def _():
        pl.semaphore_wait(barrier, 1)
        mask_down.start()
        goal_down.start()
        greet(after)

    @pl.when(tail)
    def _():
        greet(before)
        greet(beyond)


    loads = [pltpu.make_async_copy(src, dst, local_sem.at[i]) for i, (src, dst) in enumerate(pairs)]
    for load in loads:
        load.start()

    for load in loads[:3]:
        load.wait()
    eye = lax.broadcasted_iota(jnp.int32, (TAPS, 128), 0) == lax.broadcasted_iota(jnp.int32, (TAPS, 128), 1)
    ends = []
    for k in range(OWN):
        factor = jnp.sqrt(jnp.full((TAPS, TAPS), w[k], F32))
        real, imag = kr[k] * factor, ki[k] * factor
        packed[72 * k + 64 : 72 * k + 72, :] = jnp.zeros((8, 128), F32)
        packed[72 * k : 72 * k + TAPS, :] = jnp.concatenate([real[:, 0:64], imag[:, 0:64]], axis=1)
        for grid in (real, imag):
            column = jnp.broadcast_to(grid[:, 64:65], (TAPS, 128))
            ends.append(jnp.sum(jnp.where(eye, column, 0.0), axis=0, keepdims=True))
    row_id = lax.broadcasted_iota(jnp.int32, (8, 128), 0)
    end_rows = jnp.zeros((8, 128), F32)
    for i, end in enumerate(ends):
        end_rows = jnp.where(row_id == i, jnp.broadcast_to(end, (8, 128)), end_rows)
    packed[72 * OWN : 72 * OWN + 8, :] = end_rows

    @pl.when(inner)
    def _():
        pl.semaphore_wait(barrier, 3 + jnp.where(head, 0, 1) + jnp.where(eve, 1, 0))
        pl.when(turn_before)(lambda: greet(before))
        pl.when(jnp.logical_not(head))(mask_up.start)
        taps_over.start()
        pl.when(eve)(taps_on.start)
        mask_down.start()
        goal_down.start()
        pl.when(jnp.logical_not(head))(goal_up.start)

    @pl.when(eve)
    def _():
        for device in (across, mate):
            pl.semaphore_signal(relay, inc=1, device_id=device, device_id_type=MESH)
        pl.semaphore_wait(relay, 2)
        greet(after)

    def mask_of(start, count):
        row = lax.broadcasted_iota(jnp.int32, (count, COLS), 0) + (start - 64) + tile * BAND
        inside = (row >= 0) & (row < tiles * BAND)
        return jnp.where(inside, jax.nn.sigmoid(3.0 * ext[start : start + count, :]), 0.0)

    first_half = lax.broadcasted_iota(jnp.int32, (1, 128), 1) < 64

    def halves(left, right):
        return jnp.where(first_half, left, pltpu.roll(right, 64, 1))

    def square(field):
        return field[:, :128] * field[:, :128] + field[:, 128:] * field[:, 128:]

    def beside(value):
        return jnp.concatenate([value[:FX], value[FX:]], 1)

    def above(value):
        return jnp.concatenate([value[:, :128], value[:, 128:]], 0)

    def rows_in(value):
        return right_mul(beside(value), rows_c[...])

    def times_mask(which, mask_spec, group):
        mr, mi = mask_spec[:, :128], mask_spec[:, 128:]
        for k in group:
            for c in range(2):
                sr, si = spec[k, FX * c : FX * (c + 1), :128], spec[k, FX * c : FX * (c + 1), 128:]
                streams[which, k, FX * c : FX * (c + 1), :] = spread(
                    jnp.concatenate([sr * mr + si * mi, sr * mi - si * mr], 1)
                )

    def gather(which):
        real, imag = None, None
        for k in range(BOTH):
            wave = dot(streams[which, k], rows_c[...])
            for c in range(2):
                sr, si = spec[k, FX * c : FX * (c + 1), :128], spec[k, FX * c : FX * (c + 1), 128:]
                gr, gi = wave[FX * c : FX * (c + 1), :128], wave[FX * c : FX * (c + 1), 128:]
                own_real, own_imag = sr * gr - si * gi, sr * gi + si * gr
                real = own_real if real is None else real + own_real
                imag = own_imag if imag is None else imag + own_imag
        return above(right_mul(jnp.concatenate([real, imag], 1), rows_t_c[...]))

    lane = lax.broadcasted_iota(jnp.int32, (FIELD, 128), 1)

    def slope_of(which, goal_part, line):
        printed = jax.nn.sigmoid(6.0 * (part[which] + part_in[which] - 1.0))
        slope = 12.0 * (printed - goal_part) * printed * (1.0 - printed)
        line = line - RADIUS + tile * BAND
        slope = jnp.where((line >= 0) & (line < tiles * BAND), slope, 0.0)
        return jnp.concatenate([slope, slope], 1)

    def spectrum(group):
        base = group * PACK
        ends = packed[base + 72 * OWN : base + PACK, :]
        edge = edge_c[...]
        for k in range(OWN):
            taps = jnp.concatenate([packed[base + 72 * k : base + 72 * k + 72, :], jnp.zeros((56, 128), F32)], 0)
            half_way = left_mul(taps_c[...], taps, dot_t)
            for c in range(2):
                row = ends[2 * k + c : 2 * k + c + 1, :]
                own = half_way[NX * c : NX * (c + 1)] + edge * row
                streams[0, k, FX * c : FX * (c + 1), :] = spread(jnp.concatenate([own[:FX], own[FX:]], 1))
        for k in range(OWN):
            spec[group * OWN + k] = dot(streams[0, k], rows_c[...])

    for load in loads[3:6]:
        load.wait()
    spectrum(0)

    @pl.when(tail)
    def _():
        pl.semaphore_wait(barrier, 1)
        mask_up.start()
        goal_up.start()

    own_taps, other_taps = range(OWN), range(OWN, BOTH)
    for load in loads[6:10]:
        load.wait()
    mask = jnp.concatenate([mask_of(128, 64), mask_of(64, 64)], 0)
    columns[...] = left_mul(into_c[...], mask, dot_t)
    middle[...] = rows_in(columns[...])

    def block_1(group):
        times_mask(0, middle[...], group)
        for k in group:
            held[k] = dot(streams[0, k], rows_t_c[...])

    def block_2(group):
        times_mask(1, lower[...], group)
        for k in group:
            block = dot(streams[1, k], rows_t_c[...])
            for c in range(2):
                rows = slice(FX * c, FX * (c + 1))
                real = jnp.where(first_half, block[rows, :128], held[k, rows, :128])
                imag = jnp.where(first_half, block[rows, 128:], held[k, rows, 128:])
                waves[k, :, 128 * c : 128 * c + 128] = heap(jnp.concatenate([real, imag], 0))

    def begin_block_2():
        pl.when(has_after)(mask_up.wait_recv)
        mask = jnp.concatenate([jnp.zeros((64, COLS), F32), mask_of(192, 64)], 0)
        lower[...] = rows_in(jnp.where(first_half, columns[...], left_mul(into_c[...], mask, dot_t)))
        block_2(own_taps)

    def block_0():
        pl.when(has_before)(mask_down.wait_recv)
        mask = jnp.concatenate([mask_of(0, 64), jnp.zeros((64, COLS), F32)], 0)
        upper = rows_in(jnp.where(first_half, left_mul(into_c[...], mask, dot_t), columns[...]))
        times_mask(0, upper, range(BOTH))
        for k in range(BOTH):
            block = dot(streams[0, k], rows_t_c[...])
            packs[k] = halves(above(block[:FX]), above(block[FX:]))
        total = None
        for k in range(BOTH // 2):
            field = left_mul(out_c[...], jnp.concatenate([packs[2 * k], packs[2 * k + 1]], 1))
            far[k] = field
            total = square(field) if total is None else total + square(field)
        part[1] = total + pltpu.roll(total, 64, 1)
        swap_far.start()

    swap_near = send(5, part.at[0], part_in.at[0], mate)
    swap_far = send(7, part.at[1], part_in.at[1], mate)

    block_1(own_taps)
    pl.when(inner)(begin_block_2)
    taps_over.wait_recv()
    spectrum(1)
    block_1(other_taps)
    pl.when(tail)(begin_block_2)
    block_2(other_taps)
    total = None
    for k in range(BOTH):
        field = dot(out_c[...], waves[k])
        near[k] = field
        total = square(field) if total is None else total + square(field)
    part[0] = total
    swap_near.start()
    pl.when(jnp.logical_not(turn_before))(block_0)

    pl.when(has_after)(goal_up.wait_recv)
    for load in loads[10:]:
        load.wait()
    goal_near = dot_t(pick_c[...], goal[64:192, :].astype(F32).astype(BF16))
    goal_near = pltpu.roll(goal_near, 64, 1)

    swap_near.wait()
    slope = slope_of(0, goal_near, jnp.where(lane < 64, lane + 128, lane))
    for k in range(BOTH):
        begun[k] = left_mul(back_c[...], slope * near[k])
    for k in range(BOTH):
        for c in range(2):
            streams[1, k, FX * c : FX * (c + 1), :] = spread(beside(begun[k, :, 128 * c : 128 * c + 128]))
    grad_tail = gather(1)

    @pl.when(turn_before)
    def _():
        pl.semaphore_wait(barrier, 1)
        mask_up.start()
        goal_up.start()
        block_0()

    pl.when(has_before)(goal_down.wait_recv)
    goal_rows = goal[0:64, :].astype(F32).astype(BF16)
    goal_far = dot_t(pick_c[...], jnp.concatenate([goal_rows, goal_rows], 0))

    swap_far.wait()
    slope = slope_of(1, goal_far, lax.rem(lane, 64))
    for k in range(BOTH // 2):
        ended[k] = left_mul(back_c[...], slope * far[k])
    for k in range(BOTH):
        own = ended[k // 2, :, 128 * (k % 2) : 128 * (k % 2) + 128]
        for c in range(2):
            source = own if c == 0 else pltpu.roll(own, 64, 1)
            source = jnp.where(first_half, source, begun[k, :, 128 * c : 128 * c + 128])
            streams[0, k, FX * c : FX * (c + 1), :] = spread(beside(source))
    back = pltpu.roll(jnp.where(first_half, grad_tail, gather(0)), 64, 1)
    grad[...] = left_mul(last_c[...], back)
    swap_2 = send(6, grad.at[pl.ds(64, 64)], grad_in, mate)
    swap_2.start()

    own = ext[64 : 64 + BAND, :]
    own = jnp.transpose(jnp.where(half == 0, own[:, :128], own[:, 128:]))
    own = jax.nn.sigmoid(3.0 * jnp.where(core == 0, own[:64], own[64:]))
    factor = 3.0 * own * (1.0 - own)
    swap_2.wait()
    result[...] = (grad[0:64, :] + grad_in[...]) * factor
    pl.when(inner)(taps_over.wait_send)
    pl.when(eve)(taps_on.wait_send)
    for copy in (mask_down, goal_down):
        pl.when(has_after)(copy.wait_send)
    for copy in (mask_up, goal_up):
        pl.when(has_before)(copy.wait_send)


def body(consts, mask_logit, target, kern_real, kern_imag, kern_weight):
    any_spec = pl.BlockSpec(memory_space=pltpu.HBM)
    vm = pltpu.VMEM
    scratch = [
        vm((256, COLS), F32),
        vm((FROWS, COLS), jnp.int32),
        vm((OWN, TAPS, TAPS), F32),
        vm((OWN, TAPS, TAPS), F32),
        pltpu.SMEM((OWN,), F32),
        vm((2 * NX, 3 * 128), BF16),
        vm((NX, 128), F32),
        vm((768, 256), BF16),
        vm((768, 256), BF16),
        vm((NX, 3 * COLS), BF16),
        vm((FIELD, 3 * NX), BF16),
        vm((FIELD, COLS), BF16),
        vm((NX, 3 * FIELD), BF16),
        vm((128, 3 * NX), BF16),
        vm((2 * PACK, 128), F32),
        vm((BOTH, 2 * FX, 256), F32),
        vm((NX, 128), F32),
        vm((FX, 256), F32),
        vm((FX, 256), F32),
        vm((BOTH, 2 * FX, 256), F32),
        vm((2, BOTH, 2 * FX, 768), BF16),
        vm((BOTH, 3 * NX, 256), BF16),
        vm((BOTH, FIELD, 256), F32),
        vm((BOTH // 2, FIELD, 256), F32),
        vm((BOTH, 2 * FX, 128), F32),
        vm((BOTH, 2 * FX, 256), F32),
        vm((BOTH // 2, 2 * FX, 256), F32),
        vm((2, FIELD, 128), F32),
        vm((2, FIELD, 128), F32),
        vm((128, BAND), F32),
        vm((64, BAND), F32),
        pltpu.SemaphoreType.DMA((14,)),
        pltpu.SemaphoreType.DMA((9,)),
        pltpu.SemaphoreType.DMA((9,)),
        pltpu.SemaphoreType.REGULAR,
    ]
    total = pl.pallas_call(
        kernel,
        out_shape=pltpu.VMEM((64, BAND), F32),
        in_specs=[any_spec] * (5 + len(NAMES)),
        out_specs=pl.BlockSpec(memory_space=pltpu.VMEM),
        scratch_shapes=scratch,
        compiler_params=pltpu.CompilerParams(
            collective_id=0, has_side_effects=True, vmem_limit_bytes=48 * 2**20
        ),
    )(*[pltpu.with_memory_space_constraint(v, pltpu.HBM) for v in (mask_logit, target, kern_real, kern_imag, kern_weight, *consts)])
    return total.T


def solution(mesh):
    made = tables()
    consts = [made[name] for name in NAMES]
    in_specs = (
        P("tile", None),
        P("tile", None),
        P("kern", None, None),
        P("kern", None, None),
        P("kern"),
    )
    mapped = jax.shard_map(
        lambda *args: body([jnp.asarray(c) for c in consts], *args),
        mesh=mesh, in_specs=in_specs, out_specs=P("tile", "kern"), check_vma=False,
    )
    return mapped
```

time: 22.9 us -> 22.6 us (0.987)
  Pallas kernels: 22.1 us -> 21.8 us
    pallas_call x1, Pallas kernels: 22.1 us -> 21.8 us  [body(): pl.pallas_call(kernel, out_shape=pltpu.VMEM((64, BAND), F32), in_specs=[a...]
where the time goes in v4:
time: 22.6 us; the launch traced here: 22.5 us
  Pallas kernels  21.8 us (96%)
  local copies, waits for them, and re-layouts  0.62 us (3%)
    pallas_call x1, Pallas kernels, body(): pl.pallas_call(kernel, out_shape=pltpu.VMEM((64, BAND), F32), in_specs=[a...  21.8 us
    unnamed x1, local copies, waits for them, and re-layouts  0.62 us

profile of v4, /device:TPU:1, one launch (start us, length us, event | category | flops | bytes accessed | tf_op | source)
XLA Modules:
  0.0 22.5 jit_solution(15058415700426137901)
XLA Ops:
  0.0 21.8 %shard_map.136 = f32[64,128]{1,0:T(8,128)S(1)} custom-call(f32[128,256]{1,0:T(8,128)} %logit.1, s32[128,256]{1,0:T(8,128)} %target.1, f32[3,65,65]{2,1,0:T(8,128)} %kern_real.1, f32[3,65,65]{2,1,0:T(8,128)} %kern_imag.1, f32[3]{0:T(128)} %weight.1, bf16[448,384]{1,0:T(8,128)(2,1)} %constant.18.clone.taps_h, f32[224,128]{1,0:T(8,128)} %constant.19.clone.edge_h, ...), custom_call_target="tpu_custom_call" | custom-call | tf_op jit(solution)/shard_map/pallas_call | solution.py:472
  21.8 0.6 %copy.16 = f32[128,64]{0,1:T(8,128)} copy(f32[128,64]{0,1:T(8,128)S(1)} %bitcast.1) | data formatting | bytes 65536

commit v5 on v4

--- a/solution.py
+++ b/solution.py
@@ -117,7 +117,7 @@
     logit, target, kern_real, kern_imag, weight, taps_h, edge_h, rows_h, rows_t_h, into_h, out_h, pick_h, back_h, last_h,
     result,
     ext, goal, kr, ki, w, taps_c, edge_c, rows_c, rows_t_c, into_c, out_c, pick_c, back_c, last_c,
-    packed, spec, columns, middle, lower, held, streams, waves, near, far, packs, begun, ended, part, part_in, grad, grad_in,
+    packed, spare, spec, columns, middle, lower, held, streams, waves, near, far, packs, begun, ended, part, part_in, grad, grad_in,
     local_sem, send_sem, recv_sem, relay,
 ):
     tile, kern = lax.axis_index("tile"), lax.axis_index("kern")
@@ -143,12 +143,18 @@
 
     inner = jnp.logical_not(tail)
 
+    corner = tile == 0
+    served, server, giver = corner & (kern == 0), corner & (kern == 1), corner & (kern == 2)
+    beside_served = (tile == 1) & (kern == 0)
+    gives_up = jnp.logical_not(head | beside_served)
+
     @pl.when(inner)
     def _():
-        greet(across)
+        pl.when(jnp.logical_not(served))(lambda: greet(across))
+        pl.when(server)(lambda: greet({"kern": 2}))
         greet(mate)
 
-    pl.when(inner & jnp.logical_not(eve))(lambda: greet(after))
+    pl.when(inner & jnp.logical_not(eve | served))(lambda: greet(after))
     pl.when(inner & jnp.logical_not(head))(lambda: greet(before))
 
     pairs = (
@@ -178,6 +184,10 @@
     mask_up = send(1, logit.at[pl.ds(0, 64)], ext.at[pl.ds(192, 64)], before)
     taps_over = send(2, packed.at[pl.ds(0, PACK)], packed.at[pl.ds(PACK, PACK)], across)
     taps_on = send(8, packed.at[pl.ds(0, PACK)], packed.at[pl.ds(PACK, PACK)], onward, 2)
+    taps_by = send(9, packed.at[pl.ds(0, PACK)], spare, {"kern": 1}, 8)
+    mask_by = send(11, ext.at[pl.ds(192, 64)], ext.at[pl.ds(192, 64)], mate, 1)
+    goal_by = send(12, goal.at[pl.ds(160, RADIUS)], goal.at[pl.ds(160, RADIUS)], mate, 4)
+    taps_last = send(10, spare, packed.at[pl.ds(PACK, PACK)], mate, 2)
     goal_down = send(3, target.at[pl.ds(96, RADIUS)], goal.at[pl.ds(0, RADIUS)], after)
     goal_up = send(4, target.at[pl.ds(0, RADIUS)], goal.at[pl.ds(160, RADIUS)], before)
     has_before, has_after = tile > 0, tile < tiles - 1
@@ -219,14 +229,15 @@
 
     @pl.when(inner)
     def _():
-        pl.semaphore_wait(barrier, 3 + jnp.where(head, 0, 1) + jnp.where(eve, 1, 0))
+        pl.semaphore_wait(barrier, 3 + jnp.where(gives_up, 1, 0) + jnp.where(eve, 1, 0))
         pl.when(turn_before)(lambda: greet(before))
-        pl.when(jnp.logical_not(head))(mask_up.start)
-        taps_over.start()
+        pl.when(gives_up)(mask_up.start)
+        pl.when(jnp.logical_not(giver))(taps_over.start)
+        pl.when(giver)(taps_by.start)
         pl.when(eve)(taps_on.start)
         mask_down.start()
         goal_down.start()
-        pl.when(jnp.logical_not(head))(goal_up.start)
+        pl.when(gives_up)(goal_up.start)
 
     @pl.when(eve)
     def _():
@@ -301,9 +312,21 @@
         for k in range(OWN):
             spec[group * OWN + k] = dot(streams[0, k], rows_c[...])
 
+    @pl.when(server)
+    def _():
+        mask_up.wait_recv()
+        mask_by.start()
+        goal_up.wait_recv()
+        goal_by.start()
+
     for load in loads[3:6]:
         load.wait()
     spectrum(0)
+
+    @pl.when(server)
+    def _():
+        taps_by.wait_recv()
+        taps_last.start()
 
     @pl.when(tail)
     def _():
@@ -334,7 +357,7 @@
                 waves[k, :, 128 * c : 128 * c + 128] = heap(jnp.concatenate([real, imag], 0))
 
     def begin_block_2():
-        pl.when(has_after)(mask_up.wait_recv)
+        pl.when(has_after & jnp.logical_not(server))(mask_up.wait_recv)
         mask = jnp.concatenate([jnp.zeros((64, COLS), F32), mask_of(192, 64)], 0)
         lower[...] = rows_in(jnp.where(first_half, columns[...], left_mul(into_c[...], mask, dot_t)))
         block_2(own_taps)
@@ -374,7 +397,7 @@
     swap_near.start()
     pl.when(jnp.logical_not(turn_before))(block_0)
 
-    pl.when(has_after)(goal_up.wait_recv)
+    pl.when(has_after & jnp.logical_not(server))(goal_up.wait_recv)
     for load in loads[10:]:
         load.wait()
     goal_near = dot_t(pick_c[...], goal[64:192, :].astype(F32).astype(BF16))
@@ -421,12 +444,16 @@
     factor = 3.0 * own * (1.0 - own)
     swap_2.wait()
     result[...] = (grad[0:64, :] + grad_in[...]) * factor
-    pl.when(inner)(taps_over.wait_send)
+    pl.when(inner & jnp.logical_not(giver))(taps_over.wait_send)
+    pl.when(giver)(taps_by.wait_send)
+    pl.when(server)(taps_last.wait_send)
     pl.when(eve)(taps_on.wait_send)
     for copy in (mask_down, goal_down):
         pl.when(has_after)(copy.wait_send)
     for copy in (mask_up, goal_up):
-        pl.when(has_before)(copy.wait_send)
+        pl.when(has_before & jnp.logical_not(beside_served))(copy.wait_send)
+    for copy in (mask_by, goal_by):
+        pl.when(server)(copy.wait_send)
 
 
 def body(consts, mask_logit, target, kern_real, kern_imag, kern_weight):
@@ -448,6 +475,7 @@
         vm((NX, 3 * FIELD), BF16),
         vm((128, 3 * NX), BF16),
         vm((2 * PACK, 128), F32),
+        vm((PACK, 128), F32),
         vm((BOTH, 2 * FX, 256), F32),
         vm((NX, 128), F32),
         vm((FX, 256), F32),
@@ -465,8 +493,8 @@
         vm((128, BAND), F32),
         vm((64, BAND), F32),
         pltpu.SemaphoreType.DMA((14,)),
-        pltpu.SemaphoreType.DMA((9,)),
-        pltpu.SemaphoreType.DMA((9,)),
+        pltpu.SemaphoreType.DMA((13,)),
+        pltpu.SemaphoreType.DMA((13,)),
         pltpu.SemaphoreType.REGULAR,
     ]
     total = pl.pallas_call(

time: 22.6 us -> 20.7 us (0.916)
  the two profiles are of different devices: /device:TPU:1 before, /device:TPU:7 now
where the time goes in v5:
time: 20.7 us; the launch traced here: 20.6 us
  Pallas kernels  20 us (97%)
  local copies, waits for them, and re-layouts  0.62 us (3%)
    pallas_call x1, Pallas kernels, body(): pl.pallas_call(kernel, out_shape=pltpu.VMEM((64, BAND), F32), in_specs=[a...  20 us
    unnamed x1, local copies, waits for them, and re-layouts  0.62 us

profile of v5, /device:TPU:7, one launch (start us, length us, event | category | flops | bytes accessed | tf_op | source)
XLA Modules:
  0.0 20.6 jit_solution(13055830073412240930)
XLA Ops:
  0.0 20.0 %shard_map.136 = f32[64,128]{1,0:T(8,128)S(1)} custom-call(f32[128,256]{1,0:T(8,128)} %logit.1, s32[128,256]{1,0:T(8,128)} %target.1, f32[3,65,65]{2,1,0:T(8,128)} %kern_real.1, f32[3,65,65]{2,1,0:T(8,128)} %kern_imag.1, f32[3]{0:T(128)} %weight.1, bf16[448,384]{1,0:T(8,128)(2,1)} %constant.18.clone.taps_h, f32[224,128]{1,0:T(8,128)} %constant.19.clone.edge_h, ...), custom_call_target="tpu_custom_call" | custom-call | tf_op jit(solution)/shard_map/pallas_call | solution.py:500
  20.0 0.6 %copy.16 = f32[128,64]{0,1:T(8,128)} copy(f32[128,64]{0,1:T(8,128)S(1)} %bitcast.1) | data formatting | bytes 65536

commit v6 on v5

--- a/solution.py
+++ b/solution.py
@@ -231,18 +231,22 @@
     def _():
         pl.semaphore_wait(barrier, 3 + jnp.where(gives_up, 1, 0) + jnp.where(eve, 1, 0))
         pl.when(turn_before)(lambda: greet(before))
+
+        @pl.when(eve)
+        def _():
+            for device in (across, mate):
+                pl.semaphore_signal(relay, inc=1, device_id=device, device_id_type=MESH)
+            taps_on.start()
+
         pl.when(gives_up)(mask_up.start)
         pl.when(jnp.logical_not(giver))(taps_over.start)
         pl.when(giver)(taps_by.start)
-        pl.when(eve)(taps_on.start)
         mask_down.start()
         goal_down.start()
         pl.when(gives_up)(goal_up.start)
 
     @pl.when(eve)
     def _():
-        for device in (across, mate):
-            pl.semaphore_signal(relay, inc=1, device_id=device, device_id_type=MESH)
         pl.semaphore_wait(relay, 2)
         greet(after)
 
@@ -302,12 +306,14 @@
         base = group * PACK
         ends = packed[base + 72 * OWN : base + PACK, :]
         edge = edge_c[...]
+        gap = jnp.zeros((56, 128), F32)
+        taps = [jnp.concatenate([packed[base + 72 * k : base + 72 * k + 72, :], gap], 0) for k in range(OWN)]
+        pair = left_mul(taps_c[...], jnp.concatenate(taps[:2], 0), dot_t)
+        half_ways = [pair[:, :128], pair[:, 128:], left_mul(taps_c[...], taps[2], dot_t)]
         for k in range(OWN):
-            taps = jnp.concatenate([packed[base + 72 * k : base + 72 * k + 72, :], jnp.zeros((56, 128), F32)], 0)
-            half_way = left_mul(taps_c[...], taps, dot_t)
             for c in range(2):
                 row = ends[2 * k + c : 2 * k + c + 1, :]
-                own = half_way[NX * c : NX * (c + 1)] + edge * row
+                own = half_ways[k][NX * c : NX * (c + 1)] + edge * row
                 streams[0, k, FX * c : FX * (c + 1), :] = spread(jnp.concatenate([own[:FX], own[FX:]], 1))
         for k in range(OWN):
             spec[group * OWN + k] = dot(streams[0, k], rows_c[...])
@@ -403,6 +409,13 @@
     goal_near = dot_t(pick_c[...], goal[64:192, :].astype(F32).astype(BF16))
     goal_near = pltpu.roll(goal_near, 64, 1)
 
+
+    @pl.when(turn_before)
+    def _():
+        pl.semaphore_wait(barrier, 1)
+        mask_up.start()
+        goal_up.start()
+
     swap_near.wait()
     slope = slope_of(0, goal_near, jnp.where(lane < 64, lane + 128, lane))
     for k in range(BOTH):
@@ -412,12 +425,7 @@
             streams[1, k, FX * c : FX * (c + 1), :] = spread(beside(begun[k, :, 128 * c : 128 * c + 128]))
     grad_tail = gather(1)
 
-    @pl.when(turn_before)
-    def _():
-        pl.semaphore_wait(barrier, 1)
-        mask_up.start()
-        goal_up.start()
-        block_0()
+    pl.when(turn_before)(block_0)
 
     pl.when(has_before)(goal_down.wait_recv)
     goal_rows = goal[0:64, :].astype(F32).astype(BF16)

time: 20.7 us -> 20.7 us (level)
  the two profiles are of different devices: /device:TPU:7 before, /device:TPU:1 now
where the time goes in v6:
time: 20.7 us; the launch traced here: 20.4 us
  Pallas kernels  19.8 us (96%)
  local copies, waits for them, and re-layouts  0.62 us (3%)
    pallas_call x1, Pallas kernels, body(): pl.pallas_call(kernel, out_shape=pltpu.VMEM((64, BAND), F32), in_specs=[a...  19.8 us
    unnamed x1, local copies, waits for them, and re-layouts  0.62 us

profile of v6, /device:TPU:1, one launch (start us, length us, event | category | flops | bytes accessed | tf_op | source)
XLA Modules:
  0.0 20.4 jit_solution(457774055957106149)
XLA Ops:
  0.0 19.8 %shard_map.136 = f32[64,128]{1,0:T(8,128)S(1)} custom-call(f32[128,256]{1,0:T(8,128)} %logit.1, s32[128,256]{1,0:T(8,128)} %target.1, f32[3,65,65]{2,1,0:T(8,128)} %kern_real.1, f32[3,65,65]{2,1,0:T(8,128)} %kern_imag.1, f32[3]{0:T(128)} %weight.1, bf16[448,384]{1,0:T(8,128)(2,1)} %constant.18.clone.taps_h, f32[224,128]{1,0:T(8,128)} %constant.19.clone.edge_h, ...), custom_call_target="tpu_custom_call" | custom-call | tf_op jit(solution)/shard_map/pallas_call | solution.py:508
  19.8 0.6 %copy.16 = f32[128,64]{0,1:T(8,128)} copy(f32[128,64]{0,1:T(8,128)S(1)} %bitcast.1) | data formatting | bytes 65536

commit v7 on v5

--- a/solution.py
+++ b/solution.py
@@ -292,7 +292,8 @@
     lane = lax.broadcasted_iota(jnp.int32, (FIELD, 128), 1)
 
     def slope_of(which, goal_part, line):
-        printed = jax.nn.sigmoid(6.0 * (part[which] + part_in[which] - 1.0))
+        rows = goal_part.shape[0]
+        printed = jax.nn.sigmoid(6.0 * (part[which, 0:rows, :] + part_in[which, 0:rows, :] - 1.0))
         slope = 12.0 * (printed - goal_part) * printed * (1.0 - printed)
         line = line - RADIUS + tile * BAND
         slope = jnp.where((line >= 0) & (line < tiles * BAND), slope, 0.0)
@@ -375,11 +376,12 @@
             field = left_mul(out_c[...], jnp.concatenate([packs[2 * k], packs[2 * k + 1]], 1))
             far[k] = field
             total = square(field) if total is None else total + square(field)
-        part[1] = total + pltpu.roll(total, 64, 1)
+        total = total + pltpu.roll(total, 64, 1)
+        part[1, 0:80, :] = jnp.where(first_half, total[:80], total[80:])
         swap_far.start()
 
     swap_near = send(5, part.at[0], part_in.at[0], mate)
-    swap_far = send(7, part.at[1], part_in.at[1], mate)
+    swap_far = send(7, part.at[1, pl.ds(0, 80)], part_in.at[1, pl.ds(0, 80)], mate)
 
     block_1(own_taps)
     pl.when(inner)(begin_block_2)
@@ -424,7 +426,10 @@
     goal_far = dot_t(pick_c[...], jnp.concatenate([goal_rows, goal_rows], 0))
 
     swap_far.wait()
-    slope = slope_of(1, goal_far, lax.rem(lane, 64))
+    slope = slope_of(1, jnp.where(first_half, goal_far[:80], goal_far[80:]), lax.rem(lane[:80], 64))[:, :128]
+    turned = pltpu.roll(slope, 64, 1)
+    slope = jnp.concatenate([jnp.where(first_half, slope, turned), jnp.where(first_half, turned, slope)], 0)
+    slope = jnp.concatenate([slope, slope], 1)
     for k in range(BOTH // 2):
         ended[k] = left_mul(back_c[...], slope * far[k])
     for k in range(BOTH):

time: 20.7 us -> 20.8 us (level)
  the two profiles are of different devices: /device:TPU:7 before, /device:TPU:1 now
where the time goes in v7:
time: 20.8 us; the launch traced here: 20.4 us
  Pallas kernels  19.8 us (95%)
  local copies, waits for them, and re-layouts  0.62 us (3%)
    pallas_call x1, Pallas kernels, body(): pl.pallas_call(kernel, out_shape=pltpu.VMEM((64, BAND), F32), in_specs=[a...  19.8 us
    unnamed x1, local copies, waits for them, and re-layouts  0.62 us

profile of v7, /device:TPU:1, one launch (start us, length us, event | category | flops | bytes accessed | tf_op | source)
XLA Modules:
  0.0 20.4 jit_solution(13146288734267804314)
XLA Ops:
  0.0 19.8 %shard_map.136 = f32[64,128]{1,0:T(8,128)S(1)} custom-call(f32[128,256]{1,0:T(8,128)} %logit.1, s32[128,256]{1,0:T(8,128)} %target.1, f32[3,65,65]{2,1,0:T(8,128)} %kern_real.1, f32[3,65,65]{2,1,0:T(8,128)} %kern_imag.1, f32[3]{0:T(128)} %weight.1, bf16[448,384]{1,0:T(8,128)(2,1)} %constant.18.clone.taps_h, f32[224,128]{1,0:T(8,128)} %constant.19.clone.edge_h, ...), custom_call_target="tpu_custom_call" | custom-call | tf_op jit(solution)/shard_map/pallas_call | solution.py:505
  19.8 0.6 %copy.16 = f32[128,64]{0,1:T(8,128)} copy(f32[128,64]{0,1:T(8,128)S(1)} %bitcast.1) | data formatting | bytes 65536
